TPU v7x, 256 devices: a whole 4x4x8 slice. The times are simulated.
256 devices in a mesh: comp: 16 (over z, core), sect: 4 (over y), slab: 4 (over x).
Axes of the slice: x: 4, y: 4, z: 8, core: 2. Of those that a mesh axis runs over, the one named last changes fastest.
Arguments:
- spectrum: float32 [1296, 256, 512], P('comp', 'slab', 'sect'), may hold values from 0 to 1
- land_mask: int32 [256, 512], P('slab', 'sect'), may hold values 0 or 1
- ice_mask: int32 [256, 512], P('slab', 'sect'), may hold values 0 or 1
- wind_u: float32 [256, 512], P('slab', 'sect'), may hold values from -6 to 6
- wind_v: float32 [256, 512], P('slab', 'sect'), may hold values from -6 to 6
- depth: float32 [256, 512], P('slab', 'sect'), may hold values from 2 to 20
Outputs:
- damped: float32 [1296, 256, 512], P('comp', 'slab', 'sect')
- level: float32 [256, 512], P('slab', 'sect')
All inputs are finite; a program needn't handle non-finite values. No bound on the sum of `land_mask` or of `ice_mask` on one device may be relied on, other than what follows from the above.
Results may differ from a plain program's by a relative error of at most 0.00011.
Values sent between devices are 32-bit elements; how exact they have to be, the bound alone decides.
A program may use at most 64 MiB of HBM per device.

v0:
```python
import math

import jax
import jax.numpy as jnp
from jax import lax
from jax.sharding import PartitionSpec as P

ND = 36
NF = 36
STEPS = 2
JAC = 4


def extended(cells, sides, width):
    for axis, dim in sides:
        count = lax.axis_size(axis)
        ends = count - 1
        head = lax.slice_in_dim(cells, 0, width, axis=dim)
        tail = lax.slice_in_dim(cells, cells.shape[dim] - width, cells.shape[dim], axis=dim)
        cells = jnp.concatenate(
            [
                lax.ppermute(tail, axis, [(i, (i + 1) % count) for i in range(ends)]),
                cells,
                lax.ppermute(head, axis, [((i + 1) % count, i) for i in range(ends)]),
            ],
            axis=dim,
        )
    return cells


def tables(index):
    freq_index = (index // ND).astype(jnp.float32)
    angle_index = (index % ND).astype(jnp.float32)
    heading = 2.0 * math.pi * angle_index / ND
    return (
        jnp.cos(heading),
        jnp.sin(heading),
        jnp.power(1.1, -freq_index),
        jnp.power(1.1, freq_index - (NF - 1)),
        0.5 + 0.5 * freq_index / (NF - 1),
    )


def column(values):
    return values[:, None, None]


def advect(spectra, wet_cells, speed_x, speed_y):
    padded = extended(spectra, (("slab", 1), ("sect", 2)), 1)
    upper_rows = padded[:, :-2, 1:-1]
    lower_rows = padded[:, 2:, 1:-1]
    left_cells = padded[:, 1:-1, :-2]
    right_cells = padded[:, 1:-1, 2:]
    change = (
        jnp.maximum(speed_x, 0.0) * (spectra - upper_rows)
        + jnp.minimum(speed_x, 0.0) * (lower_rows - spectra)
        + jnp.maximum(speed_y, 0.0) * (spectra - left_cells)
        + jnp.minimum(speed_y, 0.0) * (right_cells - spectra)
    )
    return (spectra - change) * wet_cells


def forcing(spectra, energy, wind_east, wind_north, ice_cover, cosine, sine, high_ratio):
    project = cosine * wind_east + sine * wind_north
    growth = 0.5 * high_ratio * jnp.square(jnp.maximum(project, 0.0)) * (1.0 - ice_cover)
    return spectra * (1.0 + growth) / (1.0 + 2.0 * high_ratio * jnp.square(energy))


def stress_weights(cosine, sine, shoaling):
    return jnp.stack(
        [shoaling * (cosine * cosine + 1.0) - 0.5, shoaling * (sine * sine + 1.0) - 0.5]
    )


def surge_solve(stress):
    padded = extended(stress, (("slab", 1), ("sect", 2)), 1)
    source_term = -(
        padded[0, 2:, 1:-1]
        + padded[0, :-2, 1:-1]
        - 2.0 * stress[0]
        + (padded[1, 1:-1, 2:] + padded[1, 1:-1, :-2] - 2.0 * stress[1])
    )
    surge_level = source_term / 4.5
    for _ in range(JAC):
        neighbours = extended(surge_level, (("slab", 0), ("sect", 1)), 1)
        surge_level = (
            source_term
            + neighbours[2:, 1:-1]
            + neighbours[:-2, 1:-1]
            + neighbours[1:-1, 2:]
            + neighbours[1:-1, :-2]
        ) / 4.5
    return surge_level


def local(spectrum, land_mask, ice_mask, wind_u, wind_v, depth):
    groups = lax.axis_size("comp")
    member = lax.axis_index("comp")
    local_comp, block_rows, block_cols = spectrum.shape
    point_rows = block_rows // groups
    total_comp = ND * NF
    wet_cells = (1 - land_mask).astype(jnp.float32)
    ice_cover = ice_mask.astype(jnp.float32)

    def own_rows(values):
        return lax.dynamic_slice_in_dim(values, member * point_rows, point_rows, values.ndim - 2)

    own_index = member * local_comp + jnp.arange(local_comp, dtype=jnp.int32)
    cosine, sine, low_ratio, high_ratio, shoaling = tables(own_index)
    spectra = spectrum * wet_cells
    for _ in range(STEPS):
        spectra = advect(
            spectra, wet_cells, column(0.7 * low_ratio * cosine), column(0.7 * low_ratio * sine)
        )
    points = lax.all_to_all(spectra, "comp", split_axis=1, concat_axis=0, tiled=True)
    cosine_full, sine_full, _, high_full, shoal_full = tables(
        jnp.arange(total_comp, dtype=jnp.int32)
    )
    energy = jnp.sum(points, axis=0) / total_comp
    sourced = forcing(
        points,
        energy,
        own_rows(wind_u),
        own_rows(wind_v),
        own_rows(ice_cover),
        column(cosine_full),
        column(sine_full),
        column(high_full),
    )
    stress = (
        jnp.einsum(
            "sk,krc->src",
            stress_weights(cosine_full, sine_full, shoal_full),
            sourced,
            precision=lax.Precision.HIGHEST,
        )
        / total_comp
    )
    stress_block = lax.all_gather(stress, "comp", axis=1, tiled=True)
    level_block = surge_solve(stress_block)
    final_energy = jnp.sum(sourced, axis=0) / total_comp
    damped = sourced / (
        1.0 + 4.0 * final_energy / (jnp.square(own_rows(depth) + own_rows(level_block)) + 1.0)
    )
    result = lax.all_to_all(damped, "comp", split_axis=0, concat_axis=1, tiled=True)
    return (result, level_block)


def solution(mesh):
    in_specs = (
        P("comp", "slab", "sect"),
        P("slab", "sect"),
        P("slab", "sect"),
        P("slab", "sect"),
        P("slab", "sect"),
        P("slab", "sect"),
    )
    out_specs = (P("comp", "slab", "sect"), P("slab", "sect"))
    return jax.shard_map(local, mesh=mesh, in_specs=in_specs, out_specs=out_specs, check_vma=False)
```

profile of v0, /device:TPU:1, one launch (start us, length us, event | category | flops | bytes accessed | tf_op | source)
XLA Modules:
  0.0 333.4 jit_solution(5386185577451109580)
XLA Ops:
  1.5 4.9 %copy.16 = f32[81,64,128]{0,1,2:T(8,128)} copy(f32[81,64,128]{2,1,0:T(8,128)} %param.6) | data formatting | bytes 5308416 | tf_op args[0]
  6.4 3.7 %broadcast_multiply_fusion = f32[81,64,128]{0,1,2:T(8,128)S(1)} fusion(f32[81,64,128]{0,1,2:T(8,128)} %copy.16, f32[64,128]{0,1:T(8,128)S(1)} %copy.15), kind=kLoop, calls=%fused_computation.52 | loop fusion | flops 663552 | bytes 5341184 | tf_op jit(solution)/shard_map/mul | solution.py:110
  12.2 3.9 %collective-permute-start = (f32[81,1,128]{0,1,2:T(1,128)S(1)}, f32[81,1,128]{0,1,2:T(1,128)S(1)}, u32[]{:S(2)}, u32[]{:S(2)}) collective-permute-start(f32[81,1,128]{0,1,2:T(1,128)S(1)} %get-tuple-element.12), channel_id=1, source_target_pairs={{0,1},{1,2},{2,3},{4,5},{5,6},{6,7},{8,9},{9,10},{10,11},{12,13},{... | collective-permute-start | bytes 124424 | tf_op jit(solution)/shard_map/ppermute | solution.py:22
  17.5 3.6 %collective-permute-done.1 = f32[81,1,128]{0,1,2:T(1,128)S(1)} collective-permute-done((f32[81,1,128]{0,1,2:T(1,128)S(1)}, f32[81,1,128]{0,1,2:T(1,128)S(1)}, u32[]{:S(2)}, u32[]{:S(2)}) %collective-permute-start.1) | collective-permute-done | bytes 41504 | tf_op jit(solution)/shard_map/ppermute | solution.py:24
  21.9 3.2 collective-permute-start.2
  26.5 3.3 %collective-permute-done.3 = f32[81,66,1]{0,1,2:T(8,128)S(1)} collective-permute-done((f32[81,66,1]{0,1,2:T(8,128)S(1)}, f32[81,66,1]{0,1,2:T(8,128)S(1)}, u32[]{:S(2)}, u32[]{:S(2)}) %collective-permute-start.3) | collective-permute-done | bytes 21416 | tf_op jit(solution)/shard_map/ppermute | solution.py:24
  29.8 6.7 %fusion.17 = f32[81,64,128]{0,1,2:T(8,128)S(1)} fusion(f32[81,64,128]{0,1,2:T(8,128)S(1)} %copy-done.2, f32[81,66,1]{0,1,2:T(8,128)S(1)} %collective-permute-done.3, f32[81,1,128]{0,1,2:T(1,128)S(1)} %collective-permute-done.1, f32[81,1,128]{0,1,2:T(1,128)S(1)} %collective-permute-done, f32[81,66,1]{0,1,2:T(8,128)S(1)} %collective-permute-done.2, ...), kind=kLoop, calls=%fused_computation.26 | loop fusion | flops 13934592 | bytes 5468192 | tf_op jit(solution)/shard_map/mul | solution.py:60
  36.7 3.1 collective-permute-start.4
  41.1 3.7 %collective-permute-done.5 = f32[81,1,128]{0,1,2:T(1,128)S(1)} collective-permute-done((f32[81,1,128]{0,1,2:T(1,128)S(1)}, f32[81,1,128]{0,1,2:T(1,128)S(1)}, u32[]{:S(2)}, u32[]{:S(2)}) %collective-permute-start.5) | collective-permute-done | bytes 41504 | tf_op jit(solution)/shard_map/ppermute | solution.py:24
  44.8 3.2 collective-permute-start.6
  49.4 3.4 %collective-permute-done.7 = f32[81,66,1]{0,1,2:T(8,128)S(1)} collective-permute-done((f32[81,66,1]{0,1,2:T(8,128)S(1)}, f32[81,66,1]{0,1,2:T(8,128)S(1)}, u32[]{:S(2)}, u32[]{:S(2)}) %collective-permute-start.7) | collective-permute-done | bytes 21416 | tf_op jit(solution)/shard_map/ppermute | solution.py:24
  52.7 7.9 %fusion.4 = f32[81,64,128]{0,1,2:T(8,128)} fusion(f32[81,64,128]{0,1,2:T(8,128)S(1)} %fusion.17, f32[81,66,1]{0,1,2:T(8,128)S(1)} %collective-permute-done.7, f32[81,1,128]{0,1,2:T(1,128)S(1)} %collective-permute-done.5, f32[81,1,128]{0,1,2:T(1,128)S(1)} %collective-permute-done.4, f32[81,66,1]{0,1,2:T(8,128)S(1)} %collective-permute-done.6, ...), kind=kLoop, calls=%fused_computation.5 | loop fusion | flops 13934592 | bytes 5468192 | tf_op jit(solution)/shard_map/mul | solution.py:60
  60.6 5.3 %copy.17 = f32[81,64,128]{2,0,1:T(8,128)} copy(f32[81,64,128]{0,1,2:T(8,128)} %fusion.4) | data formatting | bytes 5308416 | tf_op jit(solution)/shard_map/mul | solution.py:60
  66.0 14.9 %all-to-all-start = ((f32[81,64,128]{2,0,1:T(8,128)}), f32[81,64,128]{2,0,1:T(8,128)}, u32[]{:S(2)}, u32[]{:S(2)}) async-start(f32[81,64,128]{2,0,1:T(8,128)} %copy.17), calls=%async_computation | async-start | bytes 5767168 | tf_op jit(solution)/shard_map/all_to_all | solution.py:115
  81.9 64.4 %all-to-all-done = f32[81,64,128]{2,0,1:T(8,128)} async-done(((f32[81,64,128]{2,0,1:T(8,128)}), f32[81,64,128]{2,0,1:T(8,128)}, u32[]{:S(2)}, u32[]{:S(2)}) %all-to-all-start) | async-done | bytes 2654240 | tf_op jit(solution)/shard_map/all_to_all | solution.py:115
  146.3 3.2 bitcast_reduce_fusion
  149.5 7.5 %fusion.29 = (f32[1296,4,128]{2,1,0:T(4,128)S(1)}, f32[1296,4,128]{2,1,0:T(4,128)S(1)}) fusion(f32[4,128]{1,0:T(4,128)S(1)} %multiply_multiply_fusion, f32[1296]{0:T(1024)S(1)} %get-tuple-element.42, f32[4,128]{1,0:T(4,128)S(1)} %get-tuple-element.38, f32[4,128]{1,0:T(4,128)S(1)} %get-tuple-element.39, f32[1296]{0:T(1024)S(1)} %get-tuple-element.40, ...), kind=kLoop, calls=%fused_computation.50 | loop fusion | flops 7962624 | bytes 7991552 | tf_op jit(solution)/shard_map/div | solution.py:66
  158.4 16.4 %all_gather.3 = f32[2,64,128]{2,0,1:T(2,128)S(1)} all-gather(f32[2,4,128]{2,0,1:T(2,128)S(1)} %fusion.31), channel_id=1, replica_groups=mesh['comp'=16,'sect'=4,'slab'=4] {'comp'}, dimensions={1}, use_global_device_ids=true | all-gather | bytes 69632 | tf_op jit(solution)/shard_map/all_gather | solution.py:139
  174.8 2.8 collective-permute-start.9
  179.0 3.0 collective-permute-done.8
  183.4 4.0 %collective-permute-start.11 = (f32[2,66,1]{2,0,1:T(2,128)S(1)}, f32[2,66,1]{2,0,1:T(2,128)S(1)}, u32[]{:S(2)}, u32[]{:S(2)}) collective-permute-start(f32[2,66,1]{2,0,1:T(2,128)S(1)} %get-tuple-element.15), channel_id=1, source_target_pairs={{0,4},{4,8},{8,12},{1,5},{5,9},{9,13},{2,6},{6,10},{10,14},{3,7},{... | collective-permute-start | bytes 1592 | tf_op jit(solution)/shard_map/ppermute | solution.py:22
  190.3 4.0 %collective-permute-start.13 = (f32[1,128]{1,0:T(1,128)S(1)}, f32[1,128]{1,0:T(1,128)S(1)}, u32[]{:S(2)}, u32[]{:S(2)}) collective-permute-start(f32[1,128]{1,0:T(1,128)S(1)} %get-tuple-element.32), channel_id=1, source_target_pairs={{0,1},{1,2},{2,3},{4,5},{5,6},{6,7},{8,9},{9,10},{10,11},{12,13},{... | collective-permute-start | bytes 1544 | tf_op jit(solution)/shard_map/ppermute | solution.py:22
  196.4 4.3 %collective-permute-start.15 = (f32[66,1]{1,0:T(8,128)S(1)}, f32[66,1]{1,0:T(8,128)S(1)}, u32[]{:S(2)}, u32[]{:S(2)}) collective-permute-start(f32[66,1]{1,0:T(8,128)S(1)} %get-tuple-element.25), channel_id=1, source_target_pairs={{0,4},{4,8},{8,12},{1,5},{5,9},{9,13},{2,6},{6,10},{10,14},{3,7},{... | collective-permute-start | bytes 800 | tf_op jit(solution)/shard_map/ppermute | solution.py:22
  203.2 4.2 %collective-permute-start.17 = (f32[1,128]{1,0:T(1,128)S(1)}, f32[1,128]{1,0:T(1,128)S(1)}, u32[]{:S(2)}, u32[]{:S(2)}) collective-permute-start(f32[1,128]{1,0:T(1,128)S(1)} %get-tuple-element.30), channel_id=1, source_target_pairs={{0,1},{1,2},{2,3},{4,5},{5,6},{6,7},{8,9},{9,10},{10,11},{12,13},{... | collective-permute-start | bytes 1544 | tf_op jit(solution)/shard_map/ppermute | solution.py:22
  209.5 4.3 %collective-permute-start.19 = (f32[66,1]{1,0:T(8,128)S(1)}, f32[66,1]{1,0:T(8,128)S(1)}, u32[]{:S(2)}, u32[]{:S(2)}) collective-permute-start(f32[66,1]{1,0:T(8,128)S(1)} %get-tuple-element.23), channel_id=1, source_target_pairs={{0,4},{4,8},{8,12},{1,5},{5,9},{9,13},{2,6},{6,10},{10,14},{3,7},{... | collective-permute-start | bytes 800 | tf_op jit(solution)/shard_map/ppermute | solution.py:22
  216.2 4.2 %collective-permute-start.21 = (f32[1,128]{1,0:T(1,128)S(1)}, f32[1,128]{1,0:T(1,128)S(1)}, u32[]{:S(2)}, u32[]{:S(2)}) collective-permute-start(f32[1,128]{1,0:T(1,128)S(1)} %get-tuple-element.28), channel_id=1, source_target_pairs={{0,1},{1,2},{2,3},{4,5},{5,6},{6,7},{8,9},{9,10},{10,11},{12,13},{... | collective-permute-start | bytes 1544 | tf_op jit(solution)/shard_map/ppermute | solution.py:22
  222.5 4.3 %collective-permute-start.23 = (f32[66,1]{1,0:T(8,128)S(1)}, f32[66,1]{1,0:T(8,128)S(1)}, u32[]{:S(2)}, u32[]{:S(2)}) collective-permute-start(f32[66,1]{1,0:T(8,128)S(1)} %get-tuple-element.21), channel_id=1, source_target_pairs={{0,4},{4,8},{8,12},{1,5},{5,9},{9,13},{2,6},{6,10},{10,14},{3,7},{... | collective-permute-start | bytes 800 | tf_op jit(solution)/shard_map/ppermute | solution.py:22
  229.3 4.2 %collective-permute-start.25 = (f32[1,128]{1,0:T(1,128)S(1)}, f32[1,128]{1,0:T(1,128)S(1)}, u32[]{:S(2)}, u32[]{:S(2)}) collective-permute-start(f32[1,128]{1,0:T(1,128)S(1)} %get-tuple-element.26), channel_id=1, source_target_pairs={{0,1},{1,2},{2,3},{4,5},{5,6},{6,7},{8,9},{9,10},{10,11},{12,13},{... | collective-permute-start | bytes 1544 | tf_op jit(solution)/shard_map/ppermute | solution.py:22
  235.5 4.3 %collective-permute-start.27 = (f32[66,1]{1,0:T(8,128)S(1)}, f32[66,1]{1,0:T(8,128)S(1)}, u32[]{:S(2)}, u32[]{:S(2)}) collective-permute-start(f32[66,1]{1,0:T(8,128)S(1)} %get-tuple-element.19), channel_id=1, source_target_pairs={{0,4},{4,8},{8,12},{1,5},{5,9},{9,13},{2,6},{6,10},{10,14},{3,7},{... | collective-permute-start | bytes 800 | tf_op jit(solution)/shard_map/ppermute | solution.py:22
  239.9 6.6 %fusion.30 = f32[4,128]{1,0:T(4,128)S(1)} fusion(f32[81,16,4,128]{3,2,0,1:T(4,128)S(1)} %get-tuple-element.5, f32[4,128]{1,0:T(4,128)S(1)} %multiply_multiply_fusion, f32[16,81]{1,0:T(8,128)S(1)} %get-tuple-element.48, f32[4,128]{1,0:T(4,128)S(1)} %get-tuple-element.38, f32[4,128]{1,0:T(4,128)S(1)} %get-tuple-element.39, f32[16,81]{1,0:T(8,128)S(1)} %get-tuple-element.46, ...), kind=kLoop, calls=%fused_computation.51 | loop fusion | flops 8625664 | bytes 2685184 | tf_op jit(solution)/shard_map/reduce_sum | solution.py:141
  247.3 3.8 %multiply_divide_fusion = f32[1296,4,128]{2,1,0:T(4,128)S(1)} fusion(f32[1296,4,128]{2,1,0:T(4,128)S(1)} %get-tuple-element.3, f32[4,128]{1,0:T(4,128)S(1)} %fusion.94, f32[4,128]{1,0:T(4,128)S(1)} %multiply_multiply_fusion, f32[1296]{0:T(1024)S(1)} %get-tuple-element.42), kind=kLoop, calls=%fused_computation.48 | loop fusion | flops 2654208 | bytes 5317696 | tf_op jit(solution)/shard_map/div | solution.py:142
  251.0 80.1 %all_to_all.36 = f32[1296,4,128]{2,1,0:T(4,128)S(1)} all-to-all(f32[1296,4,128]{2,1,0:T(4,128)S(1)} %multiply_divide_fusion), channel_id=1, replica_groups=mesh['comp'=16,'sect'=4,'slab'=4] {'comp'}, dimensions={0} | all-to-all | bytes 5308416 | tf_op jit(solution)/shard_map/all_to_all | solution.py:145
  (87 shorter events, 35.8 us)
Async XLA Ops:
  0.6 80.2 %copy-start = (f32[64,128]{1,0:T(8,128)S(1)}, f32[64,128]{1,0:T(8,128)}, u32[]{:S(2)}) copy-start(f32[64,128]{1,0:T(8,128)} %param.9) | copy-start | bytes 98308
  12.2 5.3 %collective-permute-start = (f32[81,1,128]{0,1,2:T(1,128)S(1)}, f32[81,1,128]{0,1,2:T(1,128)S(1)}, u32[]{:S(2)}, u32[]{:S(2)}) collective-permute-start(f32[81,1,128]{0,1,2:T(1,128)S(1)} %get-tuple-element.12), channel_id=1, source_target_pairs={{0,1},{1,2},{2,3},{4,5},{5,6},{6,7},{8,9},{9,10},{10,11},{12,13},{... | collective-permute-start | bytes 124424 | tf_op jit(solution)/shard_map/ppermute | solution.py:22
  16.1 5.0 %collective-permute-start.1 = (f32[81,1,128]{0,1,2:T(1,128)S(1)}, f32[81,1,128]{0,1,2:T(1,128)S(1)}, u32[]{:S(2)}, u32[]{:S(2)}) collective-permute-start(f32[81,1,128]{0,1,2:T(1,128)S(1)} %get-tuple-element.13), channel_id=1, source_target_pairs={{1,0},{2,1},{3,2},{5,4},{6,5},{7,6},{9,8},{10,9},{11,10},{13,12},{... | collective-permute-start | bytes 124424 | tf_op jit(solution)/shard_map/ppermute | solution.py:24
  17.4 12.4 %copy-start.2 = (f32[81,64,128]{0,1,2:T(8,128)S(1)}, f32[81,64,128]{0,1,2:T(8,128)}, u32[]{:S(2)}) copy-start(f32[81,64,128]{0,1,2:T(8,128)} %copy-done.1) | copy-start | bytes 7962628
  21.9 4.6 %collective-permute-start.2 = (f32[81,66,1]{0,1,2:T(8,128)S(1)}, f32[81,66,1]{0,1,2:T(8,128)S(1)}, u32[]{:S(2)}, u32[]{:S(2)}) collective-permute-start(f32[81,66,1]{0,1,2:T(8,128)S(1)} %get-tuple-element.8), channel_id=1, source_target_pairs={{0,4},{4,8},{8,12},{1,5},{5,9},{9,13},{2,6},{6,10},{10,14},{3,7},{... | collective-permute-start | bytes 64160 | tf_op jit(solution)/shard_map/ppermute | solution.py:22
  25.1 4.7 %collective-permute-start.3 = (f32[81,66,1]{0,1,2:T(8,128)S(1)}, f32[81,66,1]{0,1,2:T(8,128)S(1)}, u32[]{:S(2)}, u32[]{:S(2)}) collective-permute-start(f32[81,66,1]{0,1,2:T(8,128)S(1)} %get-tuple-element.9), channel_id=1, source_target_pairs={{4,0},{8,4},{12,8},{5,1},{9,5},{13,9},{6,2},{10,6},{14,10},{7,3},{... | collective-permute-start | bytes 64160 | tf_op jit(solution)/shard_map/ppermute | solution.py:24
  36.7 4.4 %collective-permute-start.4 = (f32[81,1,128]{0,1,2:T(1,128)S(1)}, f32[81,1,128]{0,1,2:T(1,128)S(1)}, u32[]{:S(2)}, u32[]{:S(2)}) collective-permute-start(f32[81,1,128]{0,1,2:T(1,128)S(1)} %get-tuple-element.10), channel_id=1, source_target_pairs={{0,1},{1,2},{2,3},{4,5},{5,6},{6,7},{8,9},{9,10},{10,11},{12,13},{... | collective-permute-start | bytes 124424 | tf_op jit(solution)/shard_map/ppermute | solution.py:22
  39.8 5.0 %collective-permute-start.5 = (f32[81,1,128]{0,1,2:T(1,128)S(1)}, f32[81,1,128]{0,1,2:T(1,128)S(1)}, u32[]{:S(2)}, u32[]{:S(2)}) collective-permute-start(f32[81,1,128]{0,1,2:T(1,128)S(1)} %get-tuple-element.11), channel_id=1, source_target_pairs={{1,0},{2,1},{3,2},{5,4},{6,5},{7,6},{9,8},{10,9},{11,10},{13,12},{... | collective-permute-start | bytes 124424 | tf_op jit(solution)/shard_map/ppermute | solution.py:24
  44.8 4.5 %collective-permute-start.6 = (f32[81,66,1]{0,1,2:T(8,128)S(1)}, f32[81,66,1]{0,1,2:T(8,128)S(1)}, u32[]{:S(2)}, u32[]{:S(2)}) collective-permute-start(f32[81,66,1]{0,1,2:T(8,128)S(1)} %get-tuple-element.6), channel_id=1, source_target_pairs={{0,4},{4,8},{8,12},{1,5},{5,9},{9,13},{2,6},{6,10},{10,14},{3,7},{... | collective-permute-start | bytes 64160 | tf_op jit(solution)/shard_map/ppermute | solution.py:22
  48.0 4.7 %collective-permute-start.7 = (f32[81,66,1]{0,1,2:T(8,128)S(1)}, f32[81,66,1]{0,1,2:T(8,128)S(1)}, u32[]{:S(2)}, u32[]{:S(2)}) collective-permute-start(f32[81,66,1]{0,1,2:T(8,128)S(1)} %get-tuple-element.7), channel_id=1, source_target_pairs={{4,0},{8,4},{12,8},{5,1},{9,5},{13,9},{6,2},{10,6},{14,10},{7,3},{... | collective-permute-start | bytes 64160 | tf_op jit(solution)/shard_map/ppermute | solution.py:24
  66.0 80.3 %all-to-all-start = ((f32[81,64,128]{2,0,1:T(8,128)}), f32[81,64,128]{2,0,1:T(8,128)}, u32[]{:S(2)}, u32[]{:S(2)}) async-start(f32[81,64,128]{2,0,1:T(8,128)} %copy.17), calls=%async_computation | async-start | bytes 5767168 | tf_op jit(solution)/shard_map/all_to_all | solution.py:115
  174.8 4.1 %collective-permute-start.9 = (f32[2,1,128]{2,0,1:T(2,128)S(1)}, f32[2,1,128]{2,0,1:T(2,128)S(1)}, u32[]{:S(2)}, u32[]{:S(2)}) collective-permute-start(f32[2,1,128]{2,0,1:T(2,128)S(1)} %get-tuple-element.17), channel_id=1, source_target_pairs={{0,1},{1,2},{2,3},{4,5},{5,6},{6,7},{8,9},{9,10},{10,11},{12,13},{... | collective-permute-start | bytes 3080 | tf_op jit(solution)/shard_map/ppermute | solution.py:22
  177.6 4.3 %collective-permute-start.8 = (f32[2,1,128]{2,0,1:T(2,128)S(1)}, f32[2,1,128]{2,0,1:T(2,128)S(1)}, u32[]{:S(2)}, u32[]{:S(2)}) collective-permute-start(f32[2,1,128]{2,0,1:T(2,128)S(1)} %get-tuple-element.16), channel_id=1, source_target_pairs={{1,0},{2,1},{3,2},{5,4},{6,5},{7,6},{9,8},{10,9},{11,10},{13,12},{... | collective-permute-start | bytes 3080 | tf_op jit(solution)/shard_map/ppermute | solution.py:24
  182.1 5.3 %collective-permute-start.10 = (f32[2,66,1]{2,0,1:T(2,128)S(1)}, f32[2,66,1]{2,0,1:T(2,128)S(1)}, u32[]{:S(2)}, u32[]{:S(2)}) collective-permute-start(f32[2,66,1]{2,0,1:T(2,128)S(1)} %get-tuple-element.14), channel_id=1, source_target_pairs={{4,0},{8,4},{12,8},{5,1},{9,5},{13,9},{6,2},{10,6},{14,10},{7,3},{... | collective-permute-start | bytes 1592 | tf_op jit(solution)/shard_map/ppermute | solution.py:24
  183.4 5.3 %collective-permute-start.11 = (f32[2,66,1]{2,0,1:T(2,128)S(1)}, f32[2,66,1]{2,0,1:T(2,128)S(1)}, u32[]{:S(2)}, u32[]{:S(2)}) collective-permute-start(f32[2,66,1]{2,0,1:T(2,128)S(1)} %get-tuple-element.15), channel_id=1, source_target_pairs={{0,4},{4,8},{8,12},{1,5},{5,9},{9,13},{2,6},{6,10},{10,14},{3,7},{... | collective-permute-start | bytes 1592 | tf_op jit(solution)/shard_map/ppermute | solution.py:22
  189.0 5.3 %collective-permute-start.12 = (f32[1,128]{1,0:T(1,128)S(1)}, f32[1,128]{1,0:T(1,128)S(1)}, u32[]{:S(2)}, u32[]{:S(2)}) collective-permute-start(f32[1,128]{1,0:T(1,128)S(1)} %get-tuple-element.33), channel_id=1, source_target_pairs={{1,0},{2,1},{3,2},{5,4},{6,5},{7,6},{9,8},{10,9},{11,10},{13,12},{... | collective-permute-start | bytes 1544 | tf_op jit(solution)/shard_map/ppermute | solution.py:24
  190.3 4.7 %collective-permute-start.13 = (f32[1,128]{1,0:T(1,128)S(1)}, f32[1,128]{1,0:T(1,128)S(1)}, u32[]{:S(2)}, u32[]{:S(2)}) collective-permute-start(f32[1,128]{1,0:T(1,128)S(1)} %get-tuple-element.32), channel_id=1, source_target_pairs={{0,1},{1,2},{2,3},{4,5},{5,6},{6,7},{8,9},{9,10},{10,11},{12,13},{... | collective-permute-start | bytes 1544 | tf_op jit(solution)/shard_map/ppermute | solution.py:22
  195.1 5.6 %collective-permute-start.14 = (f32[66,1]{1,0:T(8,128)S(1)}, f32[66,1]{1,0:T(8,128)S(1)}, u32[]{:S(2)}, u32[]{:S(2)}) collective-permute-start(f32[66,1]{1,0:T(8,128)S(1)} %get-tuple-element.24), channel_id=1, source_target_pairs={{4,0},{8,4},{12,8},{5,1},{9,5},{13,9},{6,2},{10,6},{14,10},{7,3},{... | collective-permute-start | bytes 800 | tf_op jit(solution)/shard_map/ppermute | solution.py:24
  196.4 5.4 %collective-permute-start.15 = (f32[66,1]{1,0:T(8,128)S(1)}, f32[66,1]{1,0:T(8,128)S(1)}, u32[]{:S(2)}, u32[]{:S(2)}) collective-permute-start(f32[66,1]{1,0:T(8,128)S(1)} %get-tuple-element.25), channel_id=1, source_target_pairs={{0,4},{4,8},{8,12},{1,5},{5,9},{9,13},{2,6},{6,10},{10,14},{3,7},{... | collective-permute-start | bytes 800 | tf_op jit(solution)/shard_map/ppermute | solution.py:22
  201.9 5.5 %collective-permute-start.16 = (f32[1,128]{1,0:T(1,128)S(1)}, f32[1,128]{1,0:T(1,128)S(1)}, u32[]{:S(2)}, u32[]{:S(2)}) collective-permute-start(f32[1,128]{1,0:T(1,128)S(1)} %get-tuple-element.31), channel_id=1, source_target_pairs={{1,0},{2,1},{3,2},{5,4},{6,5},{7,6},{9,8},{10,9},{11,10},{13,12},{... | collective-permute-start | bytes 1544 | tf_op jit(solution)/shard_map/ppermute | solution.py:24
  203.2 4.9 %collective-permute-start.17 = (f32[1,128]{1,0:T(1,128)S(1)}, f32[1,128]{1,0:T(1,128)S(1)}, u32[]{:S(2)}, u32[]{:S(2)}) collective-permute-start(f32[1,128]{1,0:T(1,128)S(1)} %get-tuple-element.30), channel_id=1, source_target_pairs={{0,1},{1,2},{2,3},{4,5},{5,6},{6,7},{8,9},{9,10},{10,11},{12,13},{... | collective-permute-start | bytes 1544 | tf_op jit(solution)/shard_map/ppermute | solution.py:22
  208.2 5.6 %collective-permute-start.18 = (f32[66,1]{1,0:T(8,128)S(1)}, f32[66,1]{1,0:T(8,128)S(1)}, u32[]{:S(2)}, u32[]{:S(2)}) collective-permute-start(f32[66,1]{1,0:T(8,128)S(1)} %get-tuple-element.22), channel_id=1, source_target_pairs={{4,0},{8,4},{12,8},{5,1},{9,5},{13,9},{6,2},{10,6},{14,10},{7,3},{... | collective-permute-start | bytes 800 | tf_op jit(solution)/shard_map/ppermute | solution.py:24
  209.5 5.3 %collective-permute-start.19 = (f32[66,1]{1,0:T(8,128)S(1)}, f32[66,1]{1,0:T(8,128)S(1)}, u32[]{:S(2)}, u32[]{:S(2)}) collective-permute-start(f32[66,1]{1,0:T(8,128)S(1)} %get-tuple-element.23), channel_id=1, source_target_pairs={{0,4},{4,8},{8,12},{1,5},{5,9},{9,13},{2,6},{6,10},{10,14},{3,7},{... | collective-permute-start | bytes 800 | tf_op jit(solution)/shard_map/ppermute | solution.py:22
  214.9 5.5 %collective-permute-start.20 = (f32[1,128]{1,0:T(1,128)S(1)}, f32[1,128]{1,0:T(1,128)S(1)}, u32[]{:S(2)}, u32[]{:S(2)}) collective-permute-start(f32[1,128]{1,0:T(1,128)S(1)} %get-tuple-element.29), channel_id=1, source_target_pairs={{1,0},{2,1},{3,2},{5,4},{6,5},{7,6},{9,8},{10,9},{11,10},{13,12},{... | collective-permute-start | bytes 1544 | tf_op jit(solution)/shard_map/ppermute | solution.py:24
  216.2 4.9 %collective-permute-start.21 = (f32[1,128]{1,0:T(1,128)S(1)}, f32[1,128]{1,0:T(1,128)S(1)}, u32[]{:S(2)}, u32[]{:S(2)}) collective-permute-start(f32[1,128]{1,0:T(1,128)S(1)} %get-tuple-element.28), channel_id=1, source_target_pairs={{0,1},{1,2},{2,3},{4,5},{5,6},{6,7},{8,9},{9,10},{10,11},{12,13},{... | collective-permute-start | bytes 1544 | tf_op jit(solution)/shard_map/ppermute | solution.py:22
  221.2 5.7 %collective-permute-start.22 = (f32[66,1]{1,0:T(8,128)S(1)}, f32[66,1]{1,0:T(8,128)S(1)}, u32[]{:S(2)}, u32[]{:S(2)}) collective-permute-start(f32[66,1]{1,0:T(8,128)S(1)} %get-tuple-element.20), channel_id=1, source_target_pairs={{4,0},{8,4},{12,8},{5,1},{9,5},{13,9},{6,2},{10,6},{14,10},{7,3},{... | collective-permute-start | bytes 800 | tf_op jit(solution)/shard_map/ppermute | solution.py:24
  222.5 5.3 %collective-permute-start.23 = (f32[66,1]{1,0:T(8,128)S(1)}, f32[66,1]{1,0:T(8,128)S(1)}, u32[]{:S(2)}, u32[]{:S(2)}) collective-permute-start(f32[66,1]{1,0:T(8,128)S(1)} %get-tuple-element.21), channel_id=1, source_target_pairs={{0,4},{4,8},{8,12},{1,5},{5,9},{9,13},{2,6},{6,10},{10,14},{3,7},{... | collective-permute-start | bytes 800 | tf_op jit(solution)/shard_map/ppermute | solution.py:22
  228.0 5.5 %collective-permute-start.24 = (f32[1,128]{1,0:T(1,128)S(1)}, f32[1,128]{1,0:T(1,128)S(1)}, u32[]{:S(2)}, u32[]{:S(2)}) collective-permute-start(f32[1,128]{1,0:T(1,128)S(1)} %get-tuple-element.27), channel_id=1, source_target_pairs={{1,0},{2,1},{3,2},{5,4},{6,5},{7,6},{9,8},{10,9},{11,10},{13,12},{... | collective-permute-start | bytes 1544 | tf_op jit(solution)/shard_map/ppermute | solution.py:24
  229.3 4.9 %collective-permute-start.25 = (f32[1,128]{1,0:T(1,128)S(1)}, f32[1,128]{1,0:T(1,128)S(1)}, u32[]{:S(2)}, u32[]{:S(2)}) collective-permute-start(f32[1,128]{1,0:T(1,128)S(1)} %get-tuple-element.26), channel_id=1, source_target_pairs={{0,1},{1,2},{2,3},{4,5},{5,6},{6,7},{8,9},{9,10},{10,11},{12,13},{... | collective-permute-start | bytes 1544 | tf_op jit(solution)/shard_map/ppermute | solution.py:22
  234.3 12.2 %collective-permute-start.26 = (f32[66,1]{1,0:T(8,128)S(1)}, f32[66,1]{1,0:T(8,128)S(1)}, u32[]{:S(2)}, u32[]{:S(2)}) collective-permute-start(f32[66,1]{1,0:T(8,128)S(1)} %get-tuple-element.18), channel_id=1, source_target_pairs={{4,0},{8,4},{12,8},{5,1},{9,5},{13,9},{6,2},{10,6},{14,10},{7,3},{... | collective-permute-start | bytes 800 | tf_op jit(solution)/shard_map/ppermute | solution.py:24
  235.5 10.9 %collective-permute-start.27 = (f32[66,1]{1,0:T(8,128)S(1)}, f32[66,1]{1,0:T(8,128)S(1)}, u32[]{:S(2)}, u32[]{:S(2)}) collective-permute-start(f32[66,1]{1,0:T(8,128)S(1)} %get-tuple-element.19), channel_id=1, source_target_pairs={{0,4},{4,8},{8,12},{1,5},{5,9},{9,13},{2,6},{6,10},{10,14},{3,7},{... | collective-permute-start | bytes 800 | tf_op jit(solution)/shard_map/ppermute | solution.py:22
  246.6 84.6 %copy-start.3 = (f32[64,128]{1,0:T(8,128)}, f32[64,128]{1,0:T(8,128)S(1)}, u32[]{:S(2)}) copy-start(f32[64,128]{1,0:T(8,128)S(1)} %fusion.35) | copy-start | bytes 98308
  (1 other events, 2.0 us)
where the time goes:
time: 337 us; the launch traced here: 333 us
  blocking collectives  96.5 us (29%)
  waiting for transfers between devices  88.6 us (26%)
  starting transfers between devices  87 us (26%)
  other arithmetic  43.5 us (13%)
  local copies, waits for them, and re-layouts  15.2 us (5%)
    all_to_all x1, blocking collectives, local(): lax.all_to_all(damped, 'comp', split_axis=0, concat_axis=1, tiled=True)  80.1 us
    all_to_all x1, waiting for transfers between devices, local(): lax.all_to_all(spectra, 'comp', split_axis=1, concat_axis=0, tiled=True)  64.4 us
    ppermute x14, starting transfers between devices, extended(): lax.ppermute(tail, axis, [(i, (i + 1) % count) for i in range(ends)])  54 us
    ppermute x14, starting transfers between devices, extended(): lax.ppermute(head, axis, [((i + 1) % count, i) for i in range(ends)])  18.1 us
    ppermute x14, waiting for transfers between devices, extended(): lax.ppermute(head, axis, [((i + 1) % count, i) for i in range(ends)])  17 us
    all_gather x1, blocking collectives, local(): stress_block = lax.all_gather(stress, 'comp', axis=1, tiled=True)  16.4 us
    all_to_all x1, starting transfers between devices, local(): lax.all_to_all(spectra, 'comp', split_axis=1, concat_axis=0, tiled=True)  14.9 us
    mul x2, other arithmetic, advect(): return (spectra - change) * wet_cells  14.6 us
  transfers between devices with their start and end apart: 29, of which 14 were waited for; matrix products, arithmetic and copies ran while one was open for 2% of the time, Pallas kernels for 0%

commit v1 on v0

v1 whole, which is shorter than its diff:
```python
import functools
import math

import jax
import jax.numpy as jnp
import numpy as np
from jax import lax
from jax.experimental import pallas as pl
from jax.experimental.pallas import tpu as pltpu
from jax.sharding import PartitionSpec as P

ND = 36
NF = 36
K = ND * NF
JAC = 4
LOCAL = 81
GROUPS = 9
COMPS = 16
SIDE = 4
MESH = pl.DeviceIdType.MESH
HIGHEST = lax.Precision.HIGHEST

ROW_DIR = (0, 1, 1, 0)
COL_DIR = (0, 0, 1, 1)
ROW_SLOT = (0, 0, 2, 2)
COL_SLOT = (0, 2, 0, 2)
EXTRA_SLOT = 4

LANE_ROWS = 16
T_LANE = 0
T_ROW = T_LANE + 2 * LANE_ROWS
T_PICK = T_ROW + 2 * 96
T_SUM = T_PICK + 2 * 96
T_END = T_SUM + 2 * 64


def direction(index):
    heading = 2.0 * math.pi * index / ND
    return math.cos(heading), math.sin(heading)


@functools.cache
def table():
    whole = np.zeros((COMPS, T_END, 128), np.float64)
    for member in range(COMPS):
        first = member % 4
        start = 9 * member // 4
        for group in range(GROUPS):
            quad = (first + group) % 4
            turn = group // 4
            freq_slot = (first + group) // 4
            freq = start + freq_slot
            row_dir, col_dir = ROW_DIR[quad], COL_DIR[quad]
            row_slot = ROW_SLOT[quad] + turn if turn < 2 else EXTRA_SLOT
            col_slot = COL_SLOT[quad] + turn if turn < 2 else EXTRA_SLOT
            low = 1.1 ** (-freq)
            scale = math.sqrt(0.5 * 1.1 ** (freq - (NF - 1)))
            for i in range(9):
                cosine, sine = direction(9 * quad + i)
                along_x, along_y = 0.7 * low * abs(cosine), 0.7 * low * abs(sine)
                values = [1.0 - along_x - along_y, along_x, along_y, scale * cosine, scale * sine]
                row = 2 * (9 * row_slot + i)
                lane = 2 * (9 * col_slot + i)
                pair = slice(lane, lane + 2)
                at = T_LANE + LANE_ROWS * col_dir
                for v, value in enumerate(values):
                    whole[member, at + v, pair] = value
                whole[member, at + 5, pair] = 1.0 if row_dir == 0 else 0.0
                whole[member, at + 6 + freq_slot, pair] = 1.0
                whole[member, at + 9 + freq_slot, pair] = cosine * cosine
                at = T_ROW + 96 * row_dir + row
                for v, value in enumerate(values):
                    whole[member, at : at + 2, v] = value
                whole[member, at : at + 2, 5] = 1.0 if col_dir == 0 else 0.0
                near = lane + 1 if col_dir == 0 else lane
                whole[member, T_PICK + 96 * row_dir + row + row_dir, near] = 1.0
                at = T_SUM + 64 * row_dir
                for side in (0, 1):
                    out = side if row_dir == 0 else 6 + side
                    whole[member, at + 16 * freq_slot + out, row + side] = 1.0
                    whole[member, at + 16 * freq_slot + 8 + out, row + side] = cosine * cosine
                    whole[member, at + 48 + out, row + side] = 1.0
    return whole.astype(np.float32)


def power(base, exponent):
    result = jnp.float32(1.0)
    for bit in range(6):
        odd = (exponent // (2**bit)) % 2
        result = result * jnp.where(odd == 1, jnp.float32(base ** (2**bit)), jnp.float32(1.0))
    return result


def from_above(cells, above=None):
    turned = pltpu.roll(cells, 1, 1)
    if above is None:
        top = jnp.zeros((1, 8, 128), jnp.float32)
    else:
        top = pltpu.roll(above, 1, 0)[None]
    before = jnp.concatenate([top, turned[:-1]], axis=0)
    sub = lax.broadcasted_iota(jnp.int32, cells.shape, 1)
    return jnp.where(sub == 0, before, turned)


def from_below(cells, below=None):
    turned = pltpu.roll(cells, 7, 1)
    if below is None:
        bottom = jnp.zeros((1, 8, 128), jnp.float32)
    else:
        bottom = pltpu.roll(below, 7, 0)[None]
    after = jnp.concatenate([turned[1:], bottom], axis=0)
    sub = lax.broadcasted_iota(jnp.int32, cells.shape, 1)
    return jnp.where(sub == 7, after, turned)


def lanes(cells, shift):
    return pltpu.roll(cells, shift % 128, cells.ndim - 1)


def lane_index(shape):
    return lax.broadcasted_iota(jnp.int32, shape, len(shape) - 1)


def from_left(cells):
    return jnp.where(lane_index(cells.shape) == 0, 0.0, lanes(cells, 1))


def from_right(cells):
    return jnp.where(lane_index(cells.shape) == 127, 0.0, lanes(cells, 127))


def step_kernel(
    spec_ref, land_ref, ice_ref, wu_ref, wv_ref, depth_ref, table_ref,
    grown_ref, factor_ref, level_ref,
    x, land, ice, wu, wv, depth, tab, wet,
    row_send, row_recv, col_send, col_recv, corner_recv,
    acc, row_fix, col_fix,
    rs_send, rs_recv, ag_send, ag_recv,
    edge_send, edge_recv, strip_send, strip_recv, tip_recv,
    fac,
    load_sem, small_sem, out_sem,
    halo_ssem, halo_rsem, rs_ssem, rs_rsem, ag_ssem, ag_rsem, rim_ssem, rim_rsem,
):
    comp = lax.axis_index("comp")
    slab = lax.axis_index("slab")
    sect = lax.axis_index("sect")
    first = comp % 4

    def place(down, right):
        return {"slab": (slab + down + SIDE) % SIDE, "sect": (sect + right + SIDE) % SIDE}

    around = [place(a, b) for a in (-1, 0, 1) for b in (-1, 0, 1) if (a, b) != (0, 0)]
    others = [{"comp": (comp + shift) % COMPS} for shift in range(1, COMPS)]
    barrier = pltpu.get_barrier_semaphore()
    for peer in around + others:
        pl.semaphore_signal(barrier, 1, device_id=peer, device_id_type=MESH)

    small = [
        pltpu.make_async_copy(src, dst, small_sem.at[n])
        for n, (src, dst) in enumerate(
            [(land_ref, land), (ice_ref, ice), (wu_ref, wu), (wv_ref, wv), (depth_ref, depth),
             (table_ref.at[comp], tab)]
        )
    ]
    for copy in small:
        copy.start()

    def load(group):
        rows = pl.ds(9 * group, 9)
        return pltpu.make_async_copy(spec_ref.at[rows], x.at[rows], load_sem.at[group])

    for group in range(GROUPS):
        load(group).start()

    lane = lane_index((8, 128))
    lane_pair = lane // 2
    sub = lax.broadcasted_iota(jnp.int32, (8, 128), 0)
    even_lane = lane % 2 == 0
    even_sub = sub % 2 == 0

    row_send[0, 9:12] = jnp.zeros((3, 8, 128), jnp.float32)
    row_send[1, 9:12] = jnp.zeros((3, 8, 128), jnp.float32)
    acc[...] = jnp.zeros_like(acc)
    for copy in small:
        copy.wait()
    wet[...] = (1 - land[...]).astype(jnp.float32)
    open_sea = (1 - ice[...]).astype(jnp.float32)
    wu[...] = wu[...] * open_sea
    wv[...] = wv[...] * open_sea

    def group_of(quad, turn):
        return (quad - first + 4) % 4 + 4 * turn

    def pack(quad, turn, packed):
        group = group_of(quad, turn)
        row_slot = ROW_SLOT[quad] + turn if turn < 2 else EXTRA_SLOT
        col_slot = COL_SLOT[quad] + turn if turn < 2 else EXTRA_SLOT
        load(group).wait()
        for i in range(9):
            cells = x[9 * group + i]
            row = 2 * (9 * row_slot + i)
            to = (ROW_DIR[quad], row // 8, pl.ds(row % 8, 2))
            if ROW_DIR[quad] == 0:
                row_send[to] = cells[7, 6:8] * wet[7, 6:8, :]
            else:
                row_send[to] = cells[0, 0:2] * wet[0, 0:2, :]
            pair = 9 * col_slot + i
            shift = 2 * pair + 2 if COL_DIR[quad] == 0 else 2 * pair
            packed = jnp.where(lane_pair == pair, lanes(cells, shift), packed)
        return packed

    for way in (0, 1):
        packed = jnp.zeros((8, 8, 128), jnp.float32)
        for quad in range(4):
            if COL_DIR[quad] == way:
                for turn in (0, 1):
                    packed = pack(quad, turn, packed)
        col_send[way] = packed
    for quad in range(4):
        @pl.when(first == quad)
        def _(quad=quad):
            col_send[COL_DIR[quad]] = pack(quad, 2, col_send[COL_DIR[quad]])

    wet_now = wet[...]
    for way in (0, 1):
        at = 126 if way == 0 else 0
        one, two = wet_now[:, :, at : at + 1], wet_now[:, :, at + 1 : at + 2]
        pair_wet = jnp.where(even_lane, one, two)
        col_send[way] = jnp.where(lane_pair == 63, pair_wet, col_send[way] * pair_wet)
    row_send[0, 11, 2:4] = wet[7, 6:8, :]
    row_send[1, 11, 2:4] = wet[0, 0:2, :]

    pl.semaphore_wait(barrier, len(around) + len(others))

    def remote(src, dst, ssem, rsem, peer):
        return pltpu.make_async_remote_copy(
            src_ref=src, dst_ref=dst, send_sem=ssem, recv_sem=rsem, device_id=peer, device_id_type=MESH
        )

    halo = [
        remote(col_send.at[0], col_recv.at[0], halo_ssem.at[0], halo_rsem.at[0], place(0, 1)),
        remote(col_send.at[1], col_recv.at[1], halo_ssem.at[1], halo_rsem.at[1], place(0, -1)),
    ]
    for way in (0, 1):
        step = 1 if way == 0 else -1
        halo.append(
            remote(col_send.at[way, 7], corner_recv.at[way, 0], halo_ssem.at[2 + way], halo_rsem.at[2 + way],
                   place(1, step))
        )
        halo.append(
            remote(col_send.at[way, 0], corner_recv.at[way, 1], halo_ssem.at[4 + way], halo_rsem.at[4 + way],
                   place(-1, step))
        )
    halo.append(remote(row_send.at[0], row_recv.at[0], halo_ssem.at[6], halo_rsem.at[6], place(1, 0)))
    halo.append(remote(row_send.at[1], row_recv.at[1], halo_ssem.at[7], halo_rsem.at[7], place(-1, 0)))
    for copy in halo:
        copy.start()

    for quad in range(4):
        upwind_row = from_above if ROW_DIR[quad] == 0 else from_below
        upwind_col = from_left if COL_DIR[quad] == 0 else from_right

        def body(turn, carry, quad=quad, upwind_row=upwind_row, upwind_col=upwind_col):
            group = group_of(quad, turn)
            freq = (9 * comp + group) // 4
            slot = (first + group) // 4
            low = 0.7 * power(1.0 / 1.1, freq)
            scale = math.sqrt(0.5 * 1.1 ** (-(NF - 1))) * power(math.sqrt(1.1), freq)
            total_e = jnp.zeros((8, 8, 128), jnp.float32)
            total_f = jnp.zeros((8, 8, 128), jnp.float32)
            total_c = jnp.zeros((8, 8, 128), jnp.float32)
            for i in range(9):
                cosine, sine = direction(9 * quad + i)
                along_x, along_y = low * abs(cosine), low * abs(sine)
                stay = 1.0 - along_x - along_y
                cells = x[9 * group + i] * wet[...]
                for _ in range(2):
                    cells = wet[...] * (
                        stay * cells + along_x * upwind_row(cells) + along_y * upwind_col(cells)
                    )
                push = jnp.maximum((scale * cosine) * wu[...] + (scale * sine) * wv[...], 0.0)
                grown = cells + cells * (push * push)
                x[9 * group + i] = grown
                total_e += cells
                total_f += grown
                total_c += (cosine * cosine) * grown
            acc[6] += total_e
            acc[2 * slot] += total_f
            acc[2 * slot + 1] += total_c
            return carry

        lax.fori_loop(0, 2 + (first == quad).astype(jnp.int32), body, 0)

    for copy in halo:
        copy.wait_recv()

    has = {
        "up": (slab > 0).astype(jnp.float32), "down": (slab < SIDE - 1).astype(jnp.float32),
        "left": (sect > 0).astype(jnp.float32), "right": (sect < SIDE - 1).astype(jnp.float32),
    }
    col_terms = []
    for way in (0, 1):
        lane_row = lambda n: tab[T_LANE + LANE_ROWS * way + n : T_LANE + LANE_ROWS * way + n + 1, :][None]
        stay, along_x, along_y, push_u, push_v, is_up = [lane_row(n) for n in range(6)]
        side = has["left"] if way == 0 else has["right"]
        got = col_recv[way] * side
        above = corner_recv[way, 0] * (side * has["up"])
        below = corner_recv[way, 1] * (side * has["down"])
        turn = 127 if way == 0 else 1
        near, near_above, near_below = lanes(got, turn), lanes(above, turn), lanes(below, turn)
        halo_wet = got[:, :, 127:128] if way == 0 else got[:, :, 126:127]
        at_near, at_far = (0, 1) if way == 0 else (127, 126)
        wet_near, wet_far = wet_now[:, :, at_near : at_near + 1], wet_now[:, :, at_far : at_far + 1]
        up_now = jnp.where(is_up > 0.5, from_above(near, near_above), from_below(near, near_below))
        outside = halo_wet * (stay * near + along_x * up_now + along_y * got)
        one = wet_near * (along_y * near)
        up_one = jnp.where(is_up > 0.5, from_above(one), from_below(one))
        two = wet_near * (stay * one + along_x * up_one + along_y * outside)
        far = lanes(wet_far * (along_y * one), 1 if way == 0 else 127)
        fix = jnp.where(even_lane, two, far) if way == 0 else jnp.where(even_lane, far, two)
        low_at = 0 if way == 0 else 126
        wind = [
            jnp.where(even_lane, w[:, :, low_at : low_at + 1], w[:, :, low_at + 1 : low_at + 2])
            for w in (wu, wv)
        ]
        push = jnp.maximum(push_u * wind[0] + push_v * wind[1], 0.0)
        fix_grown = fix + fix * (push * push)
        col_fix[way] = fix_grown
        terms = []
        for slot in range(3):
            terms += [fix_grown * lane_row(6 + slot), fix_grown * lane_row(9 + slot)]
        terms.append(fix)
        stacked = jnp.concatenate([term.reshape(64, 128) for term in terms], axis=0)
        k_index = lax.broadcasted_iota(jnp.int32, (128, 128), 0)
        to_lane = lane_index((128, 128))
        pick = ((to_lane == k_index % 2 + low_at) & (k_index < 90)).astype(jnp.float32)
        col_terms.append(jnp.dot(stacked, pick, precision=HIGHEST, preferred_element_type=jnp.float32))
    col_sum = (col_terms[0] + col_terms[1]).reshape(7, 8, 8, 128)
    acc[...] += col_sum

    for way in (0, 1):
        at = T_ROW + 96 * way
        spread = lambda n: jnp.broadcast_to(tab[at : at + 96, n : n + 1], (96, 128)).reshape(12, 8, 128)
        stay, along_x, along_y, push_u, push_v, is_left = [spread(n) for n in range(6)]
        side = has["up"] if way == 0 else has["down"]
        got = row_recv[way] * side
        near = pltpu.roll(got, 7 if way == 0 else 1, 1)
        edge = 7 if way == 0 else 0
        left_corner = corner_recv[0, way, edge : edge + 1, :] * (side * has["left"])
        right_corner = corner_recv[1, way, edge : edge + 1, :] * (side * has["right"])
        choose = tab[T_PICK + 96 * way : T_PICK + 96 * way + 96, :].reshape(12, 8, 128)
        corner = jnp.sum(
            choose * jnp.where(is_left > 0.5, left_corner[None], right_corner[None]), axis=2, keepdims=True
        )
        halo_wet = got[11, 3:4, :] if way == 0 else got[11, 2:3, :]
        tile, near_row, far_row = (0, 0, 1) if way == 0 else (7, 7, 6)
        wet_near, wet_far = wet[tile, near_row : near_row + 1, :], wet[tile, far_row : far_row + 1, :]
        lane3 = lane_index((12, 8, 128))
        beside = jnp.where(
            is_left > 0.5,
            jnp.where(lane3 == 0, corner, lanes(near, 1)),
            jnp.where(lane3 == 127, corner, lanes(near, 127)),
        )
        outside = halo_wet * (stay * near + along_x * got + along_y * beside)
        one = wet_near * (along_x * near)
        beside_one = jnp.where(is_left > 0.5, from_left(one), from_right(one))
        two = wet_near * (stay * one + along_y * beside_one + along_x * outside)
        far = pltpu.roll(wet_far * (along_x * one), 1 if way == 0 else 7, 1)
        fix = jnp.where(even_sub, two, far) if way == 0 else jnp.where(even_sub, far, two)
        low_at = 0 if way == 0 else 6
        wind = [
            jnp.where(even_sub, w[tile, low_at : low_at + 1, :], w[tile, low_at + 1 : low_at + 2, :])
            for w in (wu, wv)
        ]
        push = jnp.maximum(push_u * wind[0] + push_v * wind[1], 0.0)
        fix_grown = fix + fix * (push * push)
        row_fix[way] = fix_grown
        at = T_SUM + 64 * way
        weights = tab[at : at + 48, 0:96]
        sum_grown = jnp.dot(weights, fix_grown.reshape(96, 128), precision=HIGHEST,
                            preferred_element_type=jnp.float32)
        sum_moved = jnp.dot(tab[at + 48 : at + 56, 0:96], fix.reshape(96, 128), precision=HIGHEST,
                            preferred_element_type=jnp.float32)
        for v in range(6):
            acc[v, tile] += sum_grown[8 * v : 8 * v + 8]
        acc[6, tile] += sum_moved

    low_half = sub < 4
    for slot in range(4):
        if slot < 3:
            one, two = acc[2 * slot], acc[2 * slot + 1]
            even_tile = jnp.where(low_half, one, pltpu.roll(two, 4, 1))
            odd_tile = jnp.where(low_half, pltpu.roll(one, 4, 1), two)
        else:
            even_tile, odd_tile = acc[6], pltpu.roll(acc[6], 4, 1)
        for tile in range(8):
            rs_send[2 * tile, 8 * slot : 8 * slot + 8] = even_tile[tile]
            rs_send[2 * tile + 1, 8 * slot : 8 * slot + 8] = odd_tile[tile]
    rs = []
    for shift in range(1, COMPS):
        peer = (comp + shift) % COMPS
        rs.append(
            remote(rs_send.at[peer, pl.ds(0, 28)], rs_recv.at[comp, pl.ds(0, 28)], rs_ssem.at[shift],
                   rs_rsem.at[shift], {"comp": peer})
        )
    for copy in rs:
        copy.start()
    rs_recv[comp] = rs_send[comp]

    def store(group):
        rows = pl.ds(9 * group, 9)
        return pltpu.make_async_copy(x.at[rows], grown_ref.at[rows], out_sem.at[group])

    def amend(quad, turn):
        group = group_of(quad, turn)
        row_slot = ROW_SLOT[quad] + turn if turn < 2 else EXTRA_SLOT
        col_slot = COL_SLOT[quad] + turn if turn < 2 else EXTRA_SLOT
        way = COL_DIR[quad]
        fixes = col_fix[way]
        inside = lane < 2 if way == 0 else lane >= 126
        for i in range(9):
            at = 9 * group + i
            pair = 2 * (9 * col_slot + i)
            moved = lanes(fixes, -pair if way == 0 else 126 - pair)
            x[at] = x[at] + jnp.where(inside, moved, 0.0)
            row = 2 * (9 * row_slot + i)
            rows = row_fix[ROW_DIR[quad], row // 8, row % 8 : row % 8 + 2, :]
            if ROW_DIR[quad] == 0:
                x[at, 0, 0:2, :] += rows
            else:
                x[at, 7, 6:8, :] += rows
        store(group).start()

    for quad in range(4):
        for turn in (0, 1):
            amend(quad, turn)
        @pl.when(first == quad)
        def _(quad=quad):
            amend(quad, 2)

    for copy in rs:
        copy.wait_recv()

    energy = rs_recv[0, 24:28, :]
    for source in range(1, COMPS):
        energy = energy + rs_recv[source, 24:28, :]
    energy = energy / K
    energy = jnp.concatenate([energy, energy], axis=0)
    square = energy * energy
    plain = jnp.zeros((8, 128), jnp.float32)
    shoaled = jnp.zeros((8, 128), jnp.float32)
    for freq in range(NF):
        part = None
        for source in range(COMPS):
            slot = freq - 9 * source // 4
            if 0 <= slot < 3:
                tile = rs_recv[source, 8 * slot : 8 * slot + 8, :]
                part = tile if part is None else part + tile
        part = part / (1.0 + (2.0 * 1.1 ** (freq - (NF - 1))) * square)
        plain = plain + part
        shoaled = shoaled + (0.5 + 0.5 * freq / (NF - 1)) * part
    turned = pltpu.roll(shoaled, 4, 0)
    final = plain / K
    stress_x = (turned + shoaled - 0.5 * plain) / K
    stress_y = (2.0 * shoaled - turned - 0.5 * plain) / K
    ag_send[0:8] = jnp.where(low_half, energy, pltpu.roll(final, 4, 0))
    ag_send[8:16] = jnp.where(low_half, stress_x, pltpu.roll(stress_y, 4, 0))
    ag = [
        remote(ag_send, ag_recv.at[comp], ag_ssem.at[shift], ag_rsem.at[shift], {"comp": (comp + shift) % COMPS})
        for shift in range(1, COMPS)
    ]
    for copy in ag:
        copy.start()
    ag_recv[comp] = ag_send[...]
    for copy in ag:
        copy.wait_recv()

    gathered = ag_recv[...].reshape(8, 2, 16, 128)

    def low_of(at):
        one, two = gathered[:, 0, at : at + 8], gathered[:, 1, at : at + 8]
        return jnp.where(low_half, one, pltpu.roll(two, 4, 1))

    def high_of(at):
        one, two = gathered[:, 0, at : at + 8], gathered[:, 1, at : at + 8]
        return jnp.where(low_half, pltpu.roll(one, 4, 1), two)

    stress_x, stress_y = low_of(8), high_of(8)

    edge_send[0] = stress_x
    edge_send[1] = stress_y
    strip_send[...] = jnp.where(
        (lane < 8) | (lane >= 120), stress_x, jnp.where(lane < 64, lanes(stress_y, 8), lanes(stress_y, 120))
    )
    rim = [
        remote(strip_send, strip_recv.at[0], rim_ssem.at[0], rim_rsem.at[0], place(0, 1)),
        remote(strip_send, strip_recv.at[1], rim_ssem.at[1], rim_rsem.at[1], place(0, -1)),
        remote(edge_send.at[:, 7], edge_recv.at[0], rim_ssem.at[2], rim_rsem.at[2], place(1, 0)),
        remote(edge_send.at[:, 0], edge_recv.at[1], rim_ssem.at[3], rim_rsem.at[3], place(-1, 0)),
        remote(strip_send.at[7], tip_recv.at[0, 0], rim_ssem.at[4], rim_rsem.at[4], place(1, 1)),
        remote(strip_send.at[7], tip_recv.at[1, 0], rim_ssem.at[5], rim_rsem.at[5], place(1, -1)),
        remote(strip_send.at[0], tip_recv.at[0, 1], rim_ssem.at[6], rim_rsem.at[6], place(-1, 1)),
        remote(strip_send.at[0], tip_recv.at[1, 1], rim_ssem.at[7], rim_rsem.at[7], place(-1, -1)),
    ]
    for copy in rim:
        copy.start()
    energy, final = low_of(0), high_of(0)
    start = (9 * comp) // 4
    high = 1.1 ** (-(NF - 1)) * power(1.1, start)
    rates = [
        1.0 / (1.0 + (2.0 * 1.1**slot * high) * (energy * energy)) for slot in range(3)
    ]
    for copy in rim:
        copy.wait_recv()

    big_lane = lane_index((80, 128))
    big_row = lax.broadcasted_iota(jnp.int32, (80, 128), 0)
    first_row = jnp.where(slab > 0, 0, 8)
    last_row = jnp.where(slab < SIDE - 1, 80, 72)
    in_rows = (big_row >= first_row) & (big_row < last_row)
    right_end = jnp.where(sect < SIDE - 1, 8, 0)
    left_start = jnp.where(sect > 0, 120, 128)
    in_strip = in_rows & ((big_lane < right_end) | (big_lane >= left_start))

    def middle(n, cells):
        return jnp.where(
            in_rows,
            jnp.concatenate([edge_recv[0, n], cells.reshape(64, 128), edge_recv[1, n]], axis=0),
            0.0,
        )

    left_strip = jnp.concatenate([tip_recv[0, 0], strip_recv[0].reshape(64, 128), tip_recv[0, 1]], axis=0)
    right_strip = jnp.concatenate([tip_recv[1, 0], strip_recv[1].reshape(64, 128), tip_recv[1, 1]], axis=0)
    xx = middle(0, stress_x)
    yy = middle(1, stress_y)
    xx_strip = jnp.where(in_strip, jnp.where(big_lane < 64, right_strip, left_strip), 0.0)
    yy_strip = jnp.where(
        in_strip, jnp.where(big_lane < 64, lanes(right_strip, 120), lanes(left_strip, 8)), 0.0
    )

    def beside(center, strip):
        center_up, strip_up = lanes(center, 127), lanes(strip, 127)
        center_down, strip_down = lanes(center, 1), lanes(strip, 1)
        last, head = big_lane == 127, big_lane == 0
        return (
            jnp.where(last, strip_up, center_up) + jnp.where(head, strip_down, center_down),
            jnp.where(last, center_up, strip_up) + jnp.where(head, center_down, strip_down),
        )

    def above_below(cells):
        return pltpu.roll(cells, 1, 0) + pltpu.roll(cells, 79, 0)

    yy_sides = beside(yy, yy_strip)
    source = jnp.where(in_rows, -((above_below(xx) - 2.0 * xx) + (yy_sides[0] - 2.0 * yy)), 0.0)
    source_strip = jnp.where(
        in_strip, -((above_below(xx_strip) - 2.0 * xx_strip) + (yy_sides[1] - 2.0 * yy_strip)), 0.0
    )
    surge, surge_strip = source / 4.5, source_strip / 4.5
    for _ in range(JAC):
        sides = beside(surge, surge_strip)
        surge, surge_strip = (
            jnp.where(in_rows, (source + above_below(surge) + sides[0]) / 4.5, 0.0),
            jnp.where(in_strip, (source_strip + above_below(surge_strip) + sides[1]) / 4.5, 0.0),
        )
    surge = surge[8:72].reshape(8, 8, 128)
    reach = depth[...] + surge
    damping = 1.0 / (1.0 + 4.0 * final / (reach * reach + 1.0))
    for slot in range(3):
        fac[slot] = rates[slot] * damping
    for group in range(GROUPS):
        factor_ref[group] = fac[(first + group) // 4]
    level_ref[...] = surge

    for group in range(GROUPS):
        store(group).wait()
    for copy in halo + rs + ag + rim:
        copy.wait_send()


def damp_kernel(grown_ref, factor_ref, level_ref, out_ref, level_out):
    for group in range(grown_ref.shape[0] // 9):
        factor = factor_ref[group]
        for i in range(9):
            out_ref[9 * group + i] = grown_ref[9 * group + i] * factor
    level_out[...] = level_ref[...]


def local(spectrum, land_mask, ice_mask, wind_u, wind_v, depth):
    f32 = jnp.float32
    block = (8, 8, 128)
    anywhere = pl.BlockSpec(memory_space=pltpu.HBM)
    vmem = pl.BlockSpec(memory_space=pltpu.VMEM)
    dma = pltpu.SemaphoreType.DMA
    grown, factor, level = pl.pallas_call(
        step_kernel,
        out_shape=(
            jax.ShapeDtypeStruct((LOCAL, *block), f32),
            jax.ShapeDtypeStruct((GROUPS, *block), f32),
            jax.ShapeDtypeStruct(block, f32),
        ),
        in_specs=[anywhere] * 7,
        out_specs=(anywhere, vmem, vmem),
        scratch_shapes=[
            pltpu.VMEM((LOCAL, *block), f32),
            pltpu.VMEM(block, jnp.int32),
            pltpu.VMEM(block, jnp.int32),
            pltpu.VMEM(block, f32),
            pltpu.VMEM(block, f32),
            pltpu.VMEM(block, f32),
            pltpu.VMEM((T_END, 128), f32),
            pltpu.VMEM(block, f32),
            pltpu.VMEM((2, 12, 8, 128), f32),
            pltpu.VMEM((2, 12, 8, 128), f32),
            pltpu.VMEM((2, *block), f32),
            pltpu.VMEM((2, *block), f32),
            pltpu.VMEM((2, 2, 8, 128), f32),
            pltpu.VMEM((7, *block), f32),
            pltpu.VMEM((2, 12, 8, 128), f32),
            pltpu.VMEM((2, *block), f32),
            pltpu.VMEM((COMPS, 32, 128), f32),
            pltpu.VMEM((COMPS, 32, 128), f32),
            pltpu.VMEM((16, 128), f32),
            pltpu.VMEM((COMPS, 16, 128), f32),
            pltpu.VMEM((2, *block), f32),
            pltpu.VMEM((2, 2, 8, 128), f32),
            pltpu.VMEM(block, f32),
            pltpu.VMEM((2, *block), f32),
            pltpu.VMEM((2, 2, 8, 128), f32),
            pltpu.VMEM((3, *block), f32),
            dma((GROUPS,)),
            dma((6,)),
            dma((GROUPS,)),
            dma((8,)),
            dma((8,)),
            dma((COMPS,)),
            dma((COMPS,)),
            dma((COMPS,)),
            dma((COMPS,)),
            dma((8,)),
            dma((8,)),
        ],
        compiler_params=pltpu.CompilerParams(
            collective_id=0, has_side_effects=True, vmem_limit_bytes=60 * 1024 * 1024
        ),
        name="wave_step",
    )(
        spectrum.reshape(LOCAL, *block),
        land_mask.reshape(block),
        ice_mask.reshape(block),
        wind_u.reshape(block),
        wind_v.reshape(block),
        depth.reshape(block),
        jnp.asarray(table()),
    )
    parts = 3
    damped, level = pl.pallas_call(
        damp_kernel,
        grid=(parts,),
        out_shape=(jax.ShapeDtypeStruct((LOCAL, *block), f32), jax.ShapeDtypeStruct(block, f32)),
        in_specs=[
            pl.BlockSpec((LOCAL // parts, *block), lambda n: (n, 0, 0, 0)),
            pl.BlockSpec((GROUPS // parts, *block), lambda n: (n, 0, 0, 0)),
            pl.BlockSpec(block, lambda n: (0, 0, 0)),
        ],
        out_specs=(
            pl.BlockSpec((LOCAL // parts, *block), lambda n: (n, 0, 0, 0)),
            pl.BlockSpec(block, lambda n: (0, 0, 0)),
        ),
        compiler_params=pltpu.CompilerParams(vmem_limit_bytes=60 * 1024 * 1024),
        name="damp",
    )(grown, factor, level)
    return damped.reshape(spectrum.shape), level.reshape(depth.shape)


def solution(mesh):
    cells = P("slab", "sect")
    spectra = P("comp", "slab", "sect")
    return jax.shard_map(
        local,
        mesh=mesh,
        in_specs=(spectra, cells, cells, cells, cells, cells),
        out_specs=(spectra, cells),
        check_vma=False,
    )
```

time: 337 us -> 40.6 us (0.12)
  blocking collectives: 96.5 us -> 0 us
  waiting for transfers between devices: 88.6 us -> 0 us
  starting transfers between devices: 87 us -> 0 us
  other arithmetic: 43.5 us -> 0 us
  Pallas kernels: 0 us -> 39.7 us
  local copies, waits for them, and re-layouts: 15.2 us -> 0 us
    all_to_all x1 -> x0, blocking collectives: 80.1 us -> none  [local(): lax.all_to_all(damped, 'comp', split_axis=0, concat_axis=1, tiled=True)]
    ppermute x28 -> x0, starting transfers between devices: 72.1 us -> none  [the longest x14 54 us: extended(): lax.ppermute(tail, axis, [(i, (i + 1) % count) for i in range(ends)])]
    all_to_all x1 -> x0, waiting for transfers between devices: 64.4 us -> none  [local(): lax.all_to_all(spectra, 'comp', split_axis=1, concat_axis=0, tiled=True)]
    pallas_call x0 -> x2, Pallas kernels: none -> 39.7 us  [the longest x1 35.6 us: local(): pl.pallas_call(step_kernel, out_shape=(jax.ShapeDtypeStruct((LOCAL, *bloc...]
    ppermute x28 -> x0, waiting for transfers between devices: 24.2 us -> none  [the longest x14 17 us: extended(): lax.ppermute(head, axis, [((i + 1) % count, i) for i in range(ends)])]
    mul x5 -> x0, other arithmetic: 18.3 us -> none  [the longest x2 14.6 us: advect(): return (spectra - change) * wet_cells]
    all_gather x1 -> x0, blocking collectives: 16.4 us -> none  [local(): stress_block = lax.all_gather(stress, 'comp', axis=1, tiled=True)]
    all_to_all x1 -> x0, starting transfers between devices: 14.9 us -> none  [local(): lax.all_to_all(spectra, 'comp', split_axis=1, concat_axis=0, tiled=True)]
  transfers between devices with their start and end apart: 29 -> 0, of which waited for: 14 -> 0; matrix products, arithmetic and copies ran while one was open for 2% -> 0% of each run, Pallas kernels for 0% -> 0%
where the time goes in v1:
time: 40.6 us; the launch traced here: 40.4 us
  Pallas kernels  39.7 us (98%)
  between operations  0.64 us (2%)
    pallas_call x1, Pallas kernels, local(): pl.pallas_call(step_kernel, out_shape=(jax.ShapeDtypeStruct((LOCAL, *bloc...  35.6 us
    pallas_call x1, Pallas kernels, local(): pl.pallas_call(damp_kernel, grid=(parts,), out_shape=(jax.ShapeDtypeStruc...  4.12 us

profile of v1, /device:TPU:1, one launch (start us, length us, event | category | flops | bytes accessed | tf_op | source)
XLA Modules:
  0.0 40.4 jit_solution(6415033277047586155)
XLA Ops:
  0.6 35.6 %wave_step.1 = (f32[81,8,8,128]{3,2,1,0:T(8,128)}, f32[9,8,8,128]{3,2,1,0:T(8,128)}, f32[8,8,128]{2,1,0:T(8,128)}) custom-call(f32[81,8,8,128]{3,2,1,0:T(8,128)} %bitcast.8, s32[8,8,128]{2,1,0:T(8,128)} %bitcast.9, s32[8,8,128]{2,1,0:T(8,128)} %bitcast.10, f32[8,8,128]{2,1,0:T(8,128)} %bitcast.11, f32[8,8,128]{2,1,0:T(8,128)} %bitcast.12, ...), custom_call_target="tpu_custom_call" | custom-call | tf_op jit(solution)/shard_map/wave_step/pallas_call | solution.py:594
  36.2 4.1 %damp.1 = (f32[81,8,8,128]{3,2,1,0:T(8,128)}, f32[8,8,128]{2,1,0:T(8,128)}) custom-call(f32[81,8,8,128]{3,2,1,0:T(8,128)} %get-tuple-element.7.grown_ref, f32[9,8,8,128]{3,2,1,0:T(8,128)} %get-tuple-element.8.factor_ref, f32[8,8,128]{2,1,0:T(8,128)} %get-tuple-element.9.level_ref), custom_call_target="tpu_custom_call" | custom-call | tf_op jit(solution)/shard_map/damp/pallas_call | solution.py:656

commit v2 on v1

--- a/solution.py
+++ b/solution.py
@@ -17,6 +17,7 @@
 GROUPS = 9
 COMPS = 16
 SIDE = 4
+FAR_FIRST = (8, 7, 9, 6, 10, 5, 11, 4, 12, 3, 13, 2, 14, 1, 15)
 MESH = pl.DeviceIdType.MESH
 HIGHEST = lax.Precision.HIGHEST
 
@@ -131,14 +132,13 @@
 
 def step_kernel(
     spec_ref, land_ref, ice_ref, wu_ref, wv_ref, depth_ref, table_ref,
-    grown_ref, factor_ref, level_ref,
-    x, land, ice, wu, wv, depth, tab, wet,
+    x, factor_ref, level_ref,
+    land, ice, wu, wv, depth, tab, wet,
     row_send, row_recv, col_send, col_recv, corner_recv,
     acc, row_fix, col_fix,
     rs_send, rs_recv, ag_send, ag_recv,
     edge_send, edge_recv, strip_send, strip_recv, tip_recv,
-    fac,
-    load_sem, small_sem, out_sem,
+    load_sem, small_sem,
     halo_ssem, halo_rsem, rs_ssem, rs_rsem, ag_ssem, ag_rsem, rim_ssem, rim_rsem,
 ):
     comp = lax.axis_index("comp")
@@ -150,9 +150,9 @@
         return {"slab": (slab + down + SIDE) % SIDE, "sect": (sect + right + SIDE) % SIDE}
 
     around = [place(a, b) for a in (-1, 0, 1) for b in (-1, 0, 1) if (a, b) != (0, 0)]
-    others = [{"comp": (comp + shift) % COMPS} for shift in range(1, COMPS)]
+    others = [{"comp": (comp + shift) % COMPS} for shift in FAR_FIRST]
     barrier = pltpu.get_barrier_semaphore()
-    for peer in around + others:
+    for peer in others + around:
         pl.semaphore_signal(barrier, 1, device_id=peer, device_id_type=MESH)
 
     small = [
@@ -169,8 +169,13 @@
         rows = pl.ds(9 * group, 9)
         return pltpu.make_async_copy(spec_ref.at[rows], x.at[rows], load_sem.at[group])
 
-    for group in range(GROUPS):
-        load(group).start()
+    def group_of(quad, turn):
+        return (quad - first + 4) % 4 + 4 * turn
+
+    order = [(0, 0), (1, 0), (0, 1), (1, 1), (2, 0), (3, 0), (2, 1), (3, 1)]
+    for quad, turn in order:
+        load(group_of(quad, turn)).start()
+    load(8).start()
 
     lane = lane_index((8, 128))
     lane_pair = lane // 2
@@ -187,9 +192,6 @@
     open_sea = (1 - ice[...]).astype(jnp.float32)
     wu[...] = wu[...] * open_sea
     wv[...] = wv[...] * open_sea
-
-    def group_of(quad, turn):
-        return (quad - first + 4) % 4 + 4 * turn
 
     def pack(quad, turn, packed):
         group = group_of(quad, turn)
@@ -211,10 +213,9 @@
 
     for way in (0, 1):
         packed = jnp.zeros((8, 8, 128), jnp.float32)
-        for quad in range(4):
+        for quad, turn in order:
             if COL_DIR[quad] == way:
-                for turn in (0, 1):
-                    packed = pack(quad, turn, packed)
+                packed = pack(quad, turn, packed)
         col_send[way] = packed
     for quad in range(4):
         @pl.when(first == quad)
@@ -397,7 +398,7 @@
             rs_send[2 * tile, 8 * slot : 8 * slot + 8] = even_tile[tile]
             rs_send[2 * tile + 1, 8 * slot : 8 * slot + 8] = odd_tile[tile]
     rs = []
-    for shift in range(1, COMPS):
+    for shift in FAR_FIRST:
         peer = (comp + shift) % COMPS
         rs.append(
             remote(rs_send.at[peer, pl.ds(0, 28)], rs_recv.at[comp, pl.ds(0, 28)], rs_ssem.at[shift],
@@ -406,10 +407,6 @@
     for copy in rs:
         copy.start()
     rs_recv[comp] = rs_send[comp]
-
-    def store(group):
-        rows = pl.ds(9 * group, 9)
-        return pltpu.make_async_copy(x.at[rows], grown_ref.at[rows], out_sem.at[group])
 
     def amend(quad, turn):
         group = group_of(quad, turn)
@@ -429,7 +426,6 @@
                 x[at, 0, 0:2, :] += rows
             else:
                 x[at, 7, 6:8, :] += rows
-        store(group).start()
 
     for quad in range(4):
         for turn in (0, 1):
@@ -463,29 +459,32 @@
     final = plain / K
     stress_x = (turned + shoaled - 0.5 * plain) / K
     stress_y = (2.0 * shoaled - turned - 0.5 * plain) / K
-    ag_send[0:8] = jnp.where(low_half, energy, pltpu.roll(final, 4, 0))
-    ag_send[8:16] = jnp.where(low_half, stress_x, pltpu.roll(stress_y, 4, 0))
+    ag_send[0] = jnp.where(low_half, stress_x, pltpu.roll(stress_y, 4, 0))
+    ag_send[1] = jnp.where(low_half, energy, pltpu.roll(final, 4, 0))
     ag = [
-        remote(ag_send, ag_recv.at[comp], ag_ssem.at[shift], ag_rsem.at[shift], {"comp": (comp + shift) % COMPS})
-        for shift in range(1, COMPS)
+        [
+            remote(ag_send.at[n], ag_recv.at[n, comp], ag_ssem.at[n, shift], ag_rsem.at[n, shift],
+                   {"comp": (comp + shift) % COMPS})
+            for shift in FAR_FIRST
+        ]
+        for n in (0, 1)
     ]
-    for copy in ag:
+    for copy in ag[0] + ag[1]:
         copy.start()
-    ag_recv[comp] = ag_send[...]
-    for copy in ag:
+    ag_recv[0, comp] = ag_send[0]
+    ag_recv[1, comp] = ag_send[1]
+    for copy in ag[0]:
         copy.wait_recv()
 
-    gathered = ag_recv[...].reshape(8, 2, 16, 128)
-
-    def low_of(at):
-        one, two = gathered[:, 0, at : at + 8], gathered[:, 1, at : at + 8]
-        return jnp.where(low_half, one, pltpu.roll(two, 4, 1))
-
-    def high_of(at):
-        one, two = gathered[:, 0, at : at + 8], gathered[:, 1, at : at + 8]
-        return jnp.where(low_half, pltpu.roll(one, 4, 1), two)
-
-    stress_x, stress_y = low_of(8), high_of(8)
+    def whole(n):
+        gathered = ag_recv[n].reshape(8, 2, 8, 128)
+        one, two = gathered[:, 0], gathered[:, 1]
+        return (
+            jnp.where(low_half, one, pltpu.roll(two, 4, 1)),
+            jnp.where(low_half, pltpu.roll(one, 4, 1), two),
+        )
+
+    stress_x, stress_y = whole(0)
 
     edge_send[0] = stress_x
     edge_send[1] = stress_y
@@ -504,7 +503,9 @@
     ]
     for copy in rim:
         copy.start()
-    energy, final = low_of(0), high_of(0)
+    for copy in ag[1]:
+        copy.wait_recv()
+    energy, final = whole(1)
     start = (9 * comp) // 4
     high = 1.1 ** (-(NF - 1)) * power(1.1, start)
     rates = [
@@ -566,42 +567,48 @@
     reach = depth[...] + surge
     damping = 1.0 / (1.0 + 4.0 * final / (reach * reach + 1.0))
     for slot in range(3):
-        fac[slot] = rates[slot] * damping
+        factor_ref[slot] = rates[slot] * damping
+    level_ref[...] = surge
+
+    for copy in halo + rs + ag[0] + ag[1] + rim:
+        copy.wait_send()
+
+
+def damp_kernel(grown_ref, factor_ref, level_ref, out_ref, level_out, x, out_sem, small_sem):
+    first = lax.axis_index("comp") % 4
+
+    def store(group):
+        rows = pl.ds(9 * group, 9)
+        return pltpu.make_async_copy(x.at[rows], out_ref.at[rows], out_sem.at[group])
+
+    surge = pltpu.make_async_copy(level_ref, level_out, small_sem.at[0])
+    surge.start()
     for group in range(GROUPS):
-        factor_ref[group] = fac[(first + group) // 4]
-    level_ref[...] = surge
-
+        factor = factor_ref[(first + group) // 4]
+        for i in range(9):
+            x[9 * group + i] = grown_ref[9 * group + i] * factor
+        store(group).start()
+    surge.wait()
     for group in range(GROUPS):
         store(group).wait()
-    for copy in halo + rs + ag + rim:
-        copy.wait_send()
-
-
-def damp_kernel(grown_ref, factor_ref, level_ref, out_ref, level_out):
-    for group in range(grown_ref.shape[0] // 9):
-        factor = factor_ref[group]
-        for i in range(9):
-            out_ref[9 * group + i] = grown_ref[9 * group + i] * factor
-    level_out[...] = level_ref[...]
 
 
 def local(spectrum, land_mask, ice_mask, wind_u, wind_v, depth):
     f32 = jnp.float32
     block = (8, 8, 128)
-    anywhere = pl.BlockSpec(memory_space=pltpu.HBM)
+    anywhere = pl.BlockSpec(memory_space=pl.ANY)
     vmem = pl.BlockSpec(memory_space=pltpu.VMEM)
     dma = pltpu.SemaphoreType.DMA
     grown, factor, level = pl.pallas_call(
         step_kernel,
         out_shape=(
-            jax.ShapeDtypeStruct((LOCAL, *block), f32),
-            jax.ShapeDtypeStruct((GROUPS, *block), f32),
-            jax.ShapeDtypeStruct(block, f32),
+            pltpu.VMEM((LOCAL, *block), f32),
+            pltpu.VMEM((3, *block), f32),
+            pltpu.VMEM(block, f32),
         ),
         in_specs=[anywhere] * 7,
-        out_specs=(anywhere, vmem, vmem),
+        out_specs=(vmem, vmem, vmem),
         scratch_shapes=[
-            pltpu.VMEM((LOCAL, *block), f32),
             pltpu.VMEM(block, jnp.int32),
             pltpu.VMEM(block, jnp.int32),
             pltpu.VMEM(block, f32),
@@ -619,56 +626,55 @@
             pltpu.VMEM((2, *block), f32),
             pltpu.VMEM((COMPS, 32, 128), f32),
             pltpu.VMEM((COMPS, 32, 128), f32),
-            pltpu.VMEM((16, 128), f32),
-            pltpu.VMEM((COMPS, 16, 128), f32),
+            pltpu.VMEM((2, 8, 128), f32),
+            pltpu.VMEM((2, COMPS, 8, 128), f32),
             pltpu.VMEM((2, *block), f32),
             pltpu.VMEM((2, 2, 8, 128), f32),
             pltpu.VMEM(block, f32),
             pltpu.VMEM((2, *block), f32),
             pltpu.VMEM((2, 2, 8, 128), f32),
-            pltpu.VMEM((3, *block), f32),
             dma((GROUPS,)),
             dma((6,)),
-            dma((GROUPS,)),
             dma((8,)),
             dma((8,)),
             dma((COMPS,)),
             dma((COMPS,)),
-            dma((COMPS,)),
-            dma((COMPS,)),
+            dma((2, COMPS)),
+            dma((2, COMPS)),
             dma((8,)),
             dma((8,)),
         ],
         compiler_params=pltpu.CompilerParams(
-            collective_id=0, has_side_effects=True, vmem_limit_bytes=60 * 1024 * 1024
+            collective_id=0, has_side_effects=True, vmem_limit_bytes=24 * 1024 * 1024
         ),
         name="wave_step",
     )(
-        spectrum.reshape(LOCAL, *block),
-        land_mask.reshape(block),
-        ice_mask.reshape(block),
-        wind_u.reshape(block),
-        wind_v.reshape(block),
-        depth.reshape(block),
-        jnp.asarray(table()),
+        *[
+            pltpu.with_memory_space_constraint(operand, pltpu.HBM)
+            for operand in (
+                spectrum.reshape(LOCAL, *block),
+                land_mask.reshape(block),
+                ice_mask.reshape(block),
+                wind_u.reshape(block),
+                wind_v.reshape(block),
+                depth.reshape(block),
+                jnp.asarray(table()),
+            )
+        ]
     )
-    parts = 3
     damped, level = pl.pallas_call(
         damp_kernel,
-        grid=(parts,),
         out_shape=(jax.ShapeDtypeStruct((LOCAL, *block), f32), jax.ShapeDtypeStruct(block, f32)),
-        in_specs=[
-            pl.BlockSpec((LOCAL // parts, *block), lambda n: (n, 0, 0, 0)),
-            pl.BlockSpec((GROUPS // parts, *block), lambda n: (n, 0, 0, 0)),
-            pl.BlockSpec(block, lambda n: (0, 0, 0)),
+        in_specs=[vmem] * 3,
+        out_specs=(anywhere, anywhere),
+        scratch_shapes=[
+            pltpu.VMEM((LOCAL, *block), f32),
+            dma((GROUPS,)),
+            dma((1,)),
         ],
-        out_specs=(
-            pl.BlockSpec((LOCAL // parts, *block), lambda n: (n, 0, 0, 0)),
-            pl.BlockSpec(block, lambda n: (0, 0, 0)),
-        ),
-        compiler_params=pltpu.CompilerParams(vmem_limit_bytes=60 * 1024 * 1024),
+        compiler_params=pltpu.CompilerParams(vmem_limit_bytes=24 * 1024 * 1024),
         name="damp",
-    )(grown, factor, level)
+    )(*[pltpu.with_memory_space_constraint(operand, pltpu.VMEM) for operand in (grown, factor, level)])
     return damped.reshape(spectrum.shape), level.reshape(depth.shape)
 
 

time: 40.6 us -> 35.7 us (0.88)
  Pallas kernels: 39.7 us -> 35 us
    pallas_call x2, Pallas kernels: 39.7 us -> 35 us  [the longest x1 33.3 us: local(): pl.pallas_call(step_kernel, out_shape=(pltpu.VMEM((LOCAL, *block), f32),...]
where the time goes in v2:
time: 35.7 us; the launch traced here: 35.6 us
  Pallas kernels  35 us (98%)
  between operations  0.64 us (2%)
    pallas_call x1, Pallas kernels, local(): pl.pallas_call(step_kernel, out_shape=(pltpu.VMEM((LOCAL, *block), f32),...  33.3 us
    pallas_call x1, Pallas kernels, local(): pl.pallas_call(damp_kernel, out_shape=(jax.ShapeDtypeStruct((LOCAL, *bloc...  1.63 us

profile of v2, /device:TPU:1, one launch (start us, length us, event | category | flops | bytes accessed | tf_op | source)
XLA Modules:
  0.0 35.6 jit_solution(13155330635914846845)
XLA Ops:
  0.6 33.3 %wave_step.1 = (f32[81,8,8,128]{3,2,1,0:T(8,128)S(1)}, f32[3,8,8,128]{3,2,1,0:T(8,128)S(1)}, f32[8,8,128]{2,1,0:T(8,128)S(1)}) custom-call(f32[81,8,8,128]{3,2,1,0:T(8,128)} %bitcast.8, s32[8,8,128]{2,1,0:T(8,128)} %bitcast.9, s32[8,8,128]{2,1,0:T(8,128)} %bitcast.10, f32[8,8,128]{2,1,0:T(8,128)} %bitcast.11, f32[8,8,128]{2,1,0:T(8,128)} %bitcast.12, ...), custom_call_target="tpu_custom_call" | custom-call | tf_op jit(solution)/shard_map/wave_step/pallas_call | solution.py:602
  34.0 1.6 %damp.1 = (f32[81,8,8,128]{3,2,1,0:T(8,128)}, f32[8,8,128]{2,1,0:T(8,128)}) custom-call(f32[81,8,8,128]{3,2,1,0:T(8,128)S(1)} %get-tuple-element.7.grown_ref, f32[3,8,8,128]{3,2,1,0:T(8,128)S(1)} %get-tuple-element.8.factor_ref, f32[8,8,128]{2,1,0:T(8,128)S(1)} %get-tuple-element.9.level_ref), custom_call_target="tpu_custom_call" | custom-call | tf_op jit(solution)/shard_map/damp/pallas_call | solution.py:665

commit v3 on v2

--- a/solution.py
+++ b/solution.py
@@ -17,7 +17,10 @@
 GROUPS = 9
 COMPS = 16
 SIDE = 4
-FAR_FIRST = (8, 7, 9, 6, 10, 5, 11, 4, 12, 3, 13, 2, 14, 1, 15)
+AFTER = 13
+FAR_FIRST = tuple(
+    (chips, other) for far in (4, 3, 2, 1) for chips in ((far, -far) if far < 4 else (far,)) for other in (0, 1)
+) + ((0, 1),)
 MESH = pl.DeviceIdType.MESH
 HIGHEST = lax.Precision.HIGHEST
 
@@ -27,12 +30,13 @@
 COL_SLOT = (0, 2, 0, 2)
 EXTRA_SLOT = 4
 
-LANE_ROWS = 16
+LANE_ROWS = 8
 T_LANE = 0
 T_ROW = T_LANE + 2 * LANE_ROWS
 T_PICK = T_ROW + 2 * 96
 T_SUM = T_PICK + 2 * 96
-T_END = T_SUM + 2 * 64
+T_COL = T_SUM + 2 * 64
+T_END = T_COL + 4 * 32
 
 
 def direction(index):
@@ -67,8 +71,12 @@
                 for v, value in enumerate(values):
                     whole[member, at + v, pair] = value
                 whole[member, at + 5, pair] = 1.0 if row_dir == 0 else 0.0
-                whole[member, at + 6 + freq_slot, pair] = 1.0
-                whole[member, at + 9 + freq_slot, pair] = cosine * cosine
+                for side in (0, 1):
+                    out = 2 + side if col_dir == 0 else side
+                    at = T_COL + 64 * col_dir
+                    whole[member, at + 4 * freq_slot + out, lane + side] = 1.0
+                    whole[member, at + 16 + 4 * freq_slot + out, lane + side] = cosine * cosine
+                    whole[member, at + 32 + 12 + out, lane + side] = 1.0
                 at = T_ROW + 96 * row_dir + row
                 for v, value in enumerate(values):
                     whole[member, at : at + 2, v] = value
@@ -135,7 +143,7 @@
     x, factor_ref, level_ref,
     land, ice, wu, wv, depth, tab, wet,
     row_send, row_recv, col_send, col_recv, corner_recv,
-    acc, row_fix, col_fix,
+    acc, row_fix, col_fix, row_coef, row_gain, col_gain,
     rs_send, rs_recv, ag_send, ag_recv,
     edge_send, edge_recv, strip_send, strip_recv, tip_recv,
     load_sem, small_sem,
@@ -150,9 +158,15 @@
         return {"slab": (slab + down + SIDE) % SIDE, "sect": (sect + right + SIDE) % SIDE}
 
     around = [place(a, b) for a in (-1, 0, 1) for b in (-1, 0, 1) if (a, b) != (0, 0)]
-    others = [{"comp": (comp + shift) % COMPS} for shift in FAR_FIRST]
+    core = comp % 2
+
+    def along(chips, other):
+        return (comp - core + 2 * chips + COMPS) % COMPS + (core + other) % 2
+
+    far_first = [along(*peer) for peer in FAR_FIRST]
+    others = [{"comp": peer} for peer in far_first]
     barrier = pltpu.get_barrier_semaphore()
-    for peer in others + around:
+    for peer in around + others:
         pl.semaphore_signal(barrier, 1, device_id=peer, device_id_type=MESH)
 
     small = [
@@ -292,6 +306,27 @@
 
         lax.fori_loop(0, 2 + (first == quad).astype(jnp.int32), body, 0)
 
+    for way in (0, 1):
+        at = T_LANE + LANE_ROWS * way
+        low_at = 0 if way == 0 else 126
+        wind = [
+            jnp.where(even_lane, w[:, :, low_at : low_at + 1], w[:, :, low_at + 1 : low_at + 2])
+            for w in (wu, wv)
+        ]
+        push = jnp.maximum(tab[at + 3 : at + 4, :][None] * wind[0] + tab[at + 4 : at + 5, :][None] * wind[1], 0.0)
+        col_gain[way] = 1.0 + push * push
+        at = T_ROW + 96 * way
+        spread = lambda n: jnp.broadcast_to(tab[at : at + 96, n : n + 1], (96, 128)).reshape(12, 8, 128)
+        for n, source in enumerate((0, 1, 2, 5)):
+            row_coef[way, n] = spread(source)
+        tile, low_at = (0, 0) if way == 0 else (7, 6)
+        wind = [
+            jnp.where(even_sub, w[tile, low_at : low_at + 1, :], w[tile, low_at + 1 : low_at + 2, :])
+            for w in (wu, wv)
+        ]
+        push = jnp.maximum(spread(3) * wind[0] + spread(4) * wind[1], 0.0)
+        row_gain[way] = 1.0 + push * push
+
     for copy in halo:
         copy.wait_recv()
 
@@ -299,10 +334,10 @@
         "up": (slab > 0).astype(jnp.float32), "down": (slab < SIDE - 1).astype(jnp.float32),
         "left": (sect > 0).astype(jnp.float32), "right": (sect < SIDE - 1).astype(jnp.float32),
     }
-    col_terms = []
+    col_terms, col_weights = [], []
     for way in (0, 1):
         lane_row = lambda n: tab[T_LANE + LANE_ROWS * way + n : T_LANE + LANE_ROWS * way + n + 1, :][None]
-        stay, along_x, along_y, push_u, push_v, is_up = [lane_row(n) for n in range(6)]
+        stay, along_x, along_y, is_up = [lane_row(n) for n in (0, 1, 2, 5)]
         side = has["left"] if way == 0 else has["right"]
         got = col_recv[way] * side
         above = corner_recv[way, 0] * (side * has["up"])
@@ -319,30 +354,26 @@
         two = wet_near * (stay * one + along_x * up_one + along_y * outside)
         far = lanes(wet_far * (along_y * one), 1 if way == 0 else 127)
         fix = jnp.where(even_lane, two, far) if way == 0 else jnp.where(even_lane, far, two)
-        low_at = 0 if way == 0 else 126
-        wind = [
-            jnp.where(even_lane, w[:, :, low_at : low_at + 1], w[:, :, low_at + 1 : low_at + 2])
-            for w in (wu, wv)
-        ]
-        push = jnp.maximum(push_u * wind[0] + push_v * wind[1], 0.0)
-        fix_grown = fix + fix * (push * push)
+        fix_grown = fix * col_gain[way]
         col_fix[way] = fix_grown
-        terms = []
-        for slot in range(3):
-            terms += [fix_grown * lane_row(6 + slot), fix_grown * lane_row(9 + slot)]
-        terms.append(fix)
-        stacked = jnp.concatenate([term.reshape(64, 128) for term in terms], axis=0)
-        k_index = lax.broadcasted_iota(jnp.int32, (128, 128), 0)
-        to_lane = lane_index((128, 128))
-        pick = ((to_lane == k_index % 2 + low_at) & (k_index < 90)).astype(jnp.float32)
-        col_terms.append(jnp.dot(stacked, pick, precision=HIGHEST, preferred_element_type=jnp.float32))
-    col_sum = (col_terms[0] + col_terms[1]).reshape(7, 8, 8, 128)
-    acc[...] += col_sum
+        col_terms += [fix_grown.reshape(64, 128), fix.reshape(64, 128)]
+        at = T_COL + 64 * way
+        col_weights += [tab[at : at + 32, :], tab[at + 32 : at + 64, :]]
+    col_weights = jnp.concatenate(
+        [jnp.concatenate(col_weights, axis=1), jnp.zeros((96, 512), jnp.float32)], axis=0
+    )
+    col_out = lax.dot_general(
+        jnp.concatenate(col_terms, axis=1), col_weights, (((1,), (1,)), ((), ())),
+        precision=HIGHEST, preferred_element_type=jnp.float32,
+    ).reshape(8, 8, 128)
+    rim_lane = (lane < 2) | (lane >= 126)
+    for slot in range(3):
+        acc[2 * slot] += jnp.where(rim_lane, lanes(col_out, 126 - 4 * slot), 0.0)
+        acc[2 * slot + 1] += jnp.where(rim_lane, lanes(col_out, 110 - 4 * slot), 0.0)
+    acc[6] += jnp.where(rim_lane, lanes(col_out, 114), 0.0)
 
     for way in (0, 1):
-        at = T_ROW + 96 * way
-        spread = lambda n: jnp.broadcast_to(tab[at : at + 96, n : n + 1], (96, 128)).reshape(12, 8, 128)
-        stay, along_x, along_y, push_u, push_v, is_left = [spread(n) for n in range(6)]
+        stay, along_x, along_y, is_left = [row_coef[way, n] for n in range(4)]
         side = has["up"] if way == 0 else has["down"]
         got = row_recv[way] * side
         near = pltpu.roll(got, 7 if way == 0 else 1, 1)
@@ -368,13 +399,7 @@
         two = wet_near * (stay * one + along_y * beside_one + along_x * outside)
         far = pltpu.roll(wet_far * (along_x * one), 1 if way == 0 else 7, 1)
         fix = jnp.where(even_sub, two, far) if way == 0 else jnp.where(even_sub, far, two)
-        low_at = 0 if way == 0 else 6
-        wind = [
-            jnp.where(even_sub, w[tile, low_at : low_at + 1, :], w[tile, low_at + 1 : low_at + 2, :])
-            for w in (wu, wv)
-        ]
-        push = jnp.maximum(push_u * wind[0] + push_v * wind[1], 0.0)
-        fix_grown = fix + fix * (push * push)
+        fix_grown = fix * row_gain[way]
         row_fix[way] = fix_grown
         at = T_SUM + 64 * way
         weights = tab[at : at + 48, 0:96]
@@ -398,11 +423,10 @@
             rs_send[2 * tile, 8 * slot : 8 * slot + 8] = even_tile[tile]
             rs_send[2 * tile + 1, 8 * slot : 8 * slot + 8] = odd_tile[tile]
     rs = []
-    for shift in FAR_FIRST:
-        peer = (comp + shift) % COMPS
+    for n, peer in enumerate(far_first):
         rs.append(
-            remote(rs_send.at[peer, pl.ds(0, 28)], rs_recv.at[comp, pl.ds(0, 28)], rs_ssem.at[shift],
-                   rs_rsem.at[shift], {"comp": peer})
+            remote(rs_send.at[peer, pl.ds(0, 28)], rs_recv.at[comp, pl.ds(0, 28)], rs_ssem.at[n],
+                   rs_rsem.at[n], {"comp": peer})
         )
     for copy in rs:
         copy.start()
@@ -434,6 +458,8 @@
         def _(quad=quad):
             amend(quad, 2)
 
+    for copy in halo + rs:
+        copy.wait_send()
     for copy in rs:
         copy.wait_recv()
 
@@ -463,17 +489,20 @@
     ag_send[1] = jnp.where(low_half, energy, pltpu.roll(final, 4, 0))
     ag = [
         [
-            remote(ag_send.at[n], ag_recv.at[n, comp], ag_ssem.at[n, shift], ag_rsem.at[n, shift],
-                   {"comp": (comp + shift) % COMPS})
-            for shift in FAR_FIRST
+            remote(ag_send.at[n], ag_recv.at[n, comp], ag_ssem.at[n, at], ag_rsem.at[n, at], {"comp": peer})
+            for at, peer in enumerate(far_first)
         ]
         for n in (0, 1)
     ]
-    for copy in ag[0] + ag[1]:
+    for copy in ag[0]:
         copy.start()
     ag_recv[0, comp] = ag_send[0]
     ag_recv[1, comp] = ag_send[1]
-    for copy in ag[0]:
+    for copy in ag[0][:AFTER:-1]:
+        copy.wait_recv()
+    for copy in ag[1]:
+        copy.start()
+    for copy in ag[0][AFTER::-1]:
         copy.wait_recv()
 
     def whole(n):
@@ -511,6 +540,8 @@
     rates = [
         1.0 / (1.0 + (2.0 * 1.1**slot * high) * (energy * energy)) for slot in range(3)
     ]
+    for copy in ag[0] + ag[1]:
+        copy.wait_send()
     for copy in rim:
         copy.wait_recv()
 
@@ -556,12 +587,12 @@
     source_strip = jnp.where(
         in_strip, -((above_below(xx_strip) - 2.0 * xx_strip) + (yy_sides[1] - 2.0 * yy_strip)), 0.0
     )
-    surge, surge_strip = source / 4.5, source_strip / 4.5
+    surge, surge_strip = source * (1.0 / 4.5), source_strip * (1.0 / 4.5)
     for _ in range(JAC):
         sides = beside(surge, surge_strip)
         surge, surge_strip = (
-            jnp.where(in_rows, (source + above_below(surge) + sides[0]) / 4.5, 0.0),
-            jnp.where(in_strip, (source_strip + above_below(surge_strip) + sides[1]) / 4.5, 0.0),
+            jnp.where(in_rows, (source + above_below(surge) + sides[0]) * (1.0 / 4.5), 0.0),
+            jnp.where(in_strip, (source_strip + above_below(surge_strip) + sides[1]) * (1.0 / 4.5), 0.0),
         )
     surge = surge[8:72].reshape(8, 8, 128)
     reach = depth[...] + surge
@@ -570,7 +601,7 @@
         factor_ref[slot] = rates[slot] * damping
     level_ref[...] = surge
 
-    for copy in halo + rs + ag[0] + ag[1] + rim:
+    for copy in rim:
         copy.wait_send()
 
 
@@ -622,6 +653,9 @@
             pltpu.VMEM((2, *block), f32),
             pltpu.VMEM((2, 2, 8, 128), f32),
             pltpu.VMEM((7, *block), f32),
+            pltpu.VMEM((2, 12, 8, 128), f32),
+            pltpu.VMEM((2, *block), f32),
+            pltpu.VMEM((2, 4, 12, 8, 128), f32),
             pltpu.VMEM((2, 12, 8, 128), f32),
             pltpu.VMEM((2, *block), f32),
             pltpu.VMEM((COMPS, 32, 128), f32),

time: 35.7 us -> 35.2 us (0.986)
  Pallas kernels: 35 us -> 34.5 us
    pallas_call x1, Pallas kernels: 33.3 us -> 32.9 us  [local(): pl.pallas_call(step_kernel, out_shape=(pltpu.VMEM((LOCAL, *block), f32),...]
where the time goes in v3:
time: 35.2 us; the launch traced here: 35.1 us
  Pallas kernels  34.5 us (98%)
  between operations  0.64 us (2%)
    pallas_call x1, Pallas kernels, local(): pl.pallas_call(step_kernel, out_shape=(pltpu.VMEM((LOCAL, *block), f32),...  32.9 us
    pallas_call x1, Pallas kernels, local(): pl.pallas_call(damp_kernel, out_shape=(jax.ShapeDtypeStruct((LOCAL, *bloc...  1.63 us

profile of v3, /device:TPU:1, one launch (start us, length us, event | category | flops | bytes accessed | tf_op | source)
XLA Modules:
  0.0 35.1 jit_solution(1285757494286787069)
XLA Ops:
  0.6 32.9 %wave_step.1 = (f32[81,8,8,128]{3,2,1,0:T(8,128)S(1)}, f32[3,8,8,128]{3,2,1,0:T(8,128)S(1)}, f32[8,8,128]{2,1,0:T(8,128)S(1)}) custom-call(f32[81,8,8,128]{3,2,1,0:T(8,128)} %bitcast.8, s32[8,8,128]{2,1,0:T(8,128)} %bitcast.9, s32[8,8,128]{2,1,0:T(8,128)} %bitcast.10, f32[8,8,128]{2,1,0:T(8,128)} %bitcast.11, f32[8,8,128]{2,1,0:T(8,128)} %bitcast.12, ...), custom_call_target="tpu_custom_call" | custom-call | tf_op jit(solution)/shard_map/wave_step/pallas_call | solution.py:633
  33.5 1.6 %damp.1 = (f32[81,8,8,128]{3,2,1,0:T(8,128)}, f32[8,8,128]{2,1,0:T(8,128)}) custom-call(f32[81,8,8,128]{3,2,1,0:T(8,128)S(1)} %get-tuple-element.7.grown_ref, f32[3,8,8,128]{3,2,1,0:T(8,128)S(1)} %get-tuple-element.8.factor_ref, f32[8,8,128]{2,1,0:T(8,128)S(1)} %get-tuple-element.9.level_ref), custom_call_target="tpu_custom_call" | custom-call | tf_op jit(solution)/shard_map/damp/pallas_call | solution.py:699

commit v4 on v3

--- a/solution.py
+++ b/solution.py
@@ -146,7 +146,7 @@
     acc, row_fix, col_fix, row_coef, row_gain, col_gain,
     rs_send, rs_recv, ag_send, ag_recv,
     edge_send, edge_recv, strip_send, strip_recv, tip_recv,
-    load_sem, small_sem,
+    relay, load_sem, small_sem,
     halo_ssem, halo_rsem, rs_ssem, rs_rsem, ag_ssem, ag_rsem, rim_ssem, rim_rsem,
 ):
     comp = lax.axis_index("comp")
@@ -164,10 +164,14 @@
         return (comp - core + 2 * chips + COMPS) % COMPS + (core + other) % 2
 
     far_first = [along(*peer) for peer in FAR_FIRST]
-    others = [{"comp": peer} for peer in far_first]
+    nearest = [{"comp": along(*peer)} for peer in ((1, 0), (-1, 0), (1, 1), (-1, 1), (0, 1))]
     barrier = pltpu.get_barrier_semaphore()
-    for peer in around + others:
+    for peer in around + nearest:
         pl.semaphore_signal(barrier, 1, device_id=peer, device_id_type=MESH)
+
+    def tell(turn, chips):
+        for peer in (along(chips, 0), along(-chips, 0)):
+            pl.semaphore_signal(relay.at[turn], 1, device_id={"comp": peer}, device_id_type=MESH)
 
     small = [
         pltpu.make_async_copy(src, dst, small_sem.at[n])
@@ -176,8 +180,7 @@
              (table_ref.at[comp], tab)]
         )
     ]
-    for copy in small:
-        copy.start()
+    small[0].start()
 
     def load(group):
         rows = pl.ds(9 * group, 9)
@@ -190,6 +193,8 @@
     for quad, turn in order:
         load(group_of(quad, turn)).start()
     load(8).start()
+    for copy in small[1:]:
+        copy.start()
 
     lane = lane_index((8, 128))
     lane_pair = lane // 2
@@ -199,13 +204,8 @@
 
     row_send[0, 9:12] = jnp.zeros((3, 8, 128), jnp.float32)
     row_send[1, 9:12] = jnp.zeros((3, 8, 128), jnp.float32)
-    acc[...] = jnp.zeros_like(acc)
-    for copy in small:
-        copy.wait()
+    small[0].wait()
     wet[...] = (1 - land[...]).astype(jnp.float32)
-    open_sea = (1 - ice[...]).astype(jnp.float32)
-    wu[...] = wu[...] * open_sea
-    wv[...] = wv[...] * open_sea
 
     def pack(quad, turn, packed):
         group = group_of(quad, turn)
@@ -245,7 +245,7 @@
     row_send[0, 11, 2:4] = wet[7, 6:8, :]
     row_send[1, 11, 2:4] = wet[0, 0:2, :]
 
-    pl.semaphore_wait(barrier, len(around) + len(others))
+    pl.semaphore_wait(barrier, len(around) + len(nearest))
 
     def remote(src, dst, ssem, rsem, peer):
         return pltpu.make_async_remote_copy(
@@ -270,6 +270,14 @@
     halo.append(remote(row_send.at[1], row_recv.at[1], halo_ssem.at[7], halo_rsem.at[7], place(-1, 0)))
     for copy in halo:
         copy.start()
+    tell(0, 1)
+
+    acc[...] = jnp.zeros_like(acc)
+    for copy in small[1:]:
+        copy.wait()
+    open_sea = (1 - ice[...]).astype(jnp.float32)
+    wu[...] = wu[...] * open_sea
+    wv[...] = wv[...] * open_sea
 
     for quad in range(4):
         upwind_row = from_above if ROW_DIR[quad] == 0 else from_below
@@ -305,6 +313,9 @@
             return carry
 
         lax.fori_loop(0, 2 + (first == quad).astype(jnp.int32), body, 0)
+        if quad == 1:
+            pl.semaphore_wait(relay.at[0], 2)
+            tell(1, 2)
 
     for way in (0, 1):
         at = T_LANE + LANE_ROWS * way
@@ -422,6 +433,7 @@
         for tile in range(8):
             rs_send[2 * tile, 8 * slot : 8 * slot + 8] = even_tile[tile]
             rs_send[2 * tile + 1, 8 * slot : 8 * slot + 8] = odd_tile[tile]
+    pl.semaphore_wait(relay.at[1], 2)
     rs = []
     for n, peer in enumerate(far_first):
         rs.append(
@@ -667,6 +679,7 @@
             pltpu.VMEM(block, f32),
             pltpu.VMEM((2, *block), f32),
             pltpu.VMEM((2, 2, 8, 128), f32),
+            pltpu.SemaphoreType.REGULAR((2,)),
             dma((GROUPS,)),
             dma((6,)),
             dma((8,)),

time: 35.2 us -> 34.4 us (0.977)
  Pallas kernels: 34.5 us -> 33.7 us
    pallas_call x1, Pallas kernels: 32.9 us -> 32.1 us  [local(): pl.pallas_call(step_kernel, out_shape=(pltpu.VMEM((LOCAL, *block), f32),...]
where the time goes in v4:
time: 34.4 us; the launch traced here: 34.3 us
  Pallas kernels  33.7 us (98%)
  between operations  0.64 us (2%)
    pallas_call x1, Pallas kernels, local(): pl.pallas_call(step_kernel, out_shape=(pltpu.VMEM((LOCAL, *block), f32),...  32.1 us
    pallas_call x1, Pallas kernels, local(): pl.pallas_call(damp_kernel, out_shape=(jax.ShapeDtypeStruct((LOCAL, *bloc...  1.63 us

profile of v4, /device:TPU:1, one launch (start us, length us, event | category | flops | bytes accessed | tf_op | source)
XLA Modules:
  0.0 34.3 jit_solution(15207083259793121274)
XLA Ops:
  0.6 32.1 %wave_step.1 = (f32[81,8,8,128]{3,2,1,0:T(8,128)S(1)}, f32[3,8,8,128]{3,2,1,0:T(8,128)S(1)}, f32[8,8,128]{2,1,0:T(8,128)S(1)}) custom-call(f32[81,8,8,128]{3,2,1,0:T(8,128)} %bitcast.8, s32[8,8,128]{2,1,0:T(8,128)} %bitcast.9, s32[8,8,128]{2,1,0:T(8,128)} %bitcast.10, f32[8,8,128]{2,1,0:T(8,128)} %bitcast.11, f32[8,8,128]{2,1,0:T(8,128)} %bitcast.12, ...), custom_call_target="tpu_custom_call" | custom-call | tf_op jit(solution)/shard_map/wave_step/pallas_call | solution.py:645
  32.7 1.6 %damp.1 = (f32[81,8,8,128]{3,2,1,0:T(8,128)}, f32[8,8,128]{2,1,0:T(8,128)}) custom-call(f32[81,8,8,128]{3,2,1,0:T(8,128)S(1)} %get-tuple-element.7.grown_ref, f32[3,8,8,128]{3,2,1,0:T(8,128)S(1)} %get-tuple-element.8.factor_ref, f32[8,8,128]{2,1,0:T(8,128)S(1)} %get-tuple-element.9.level_ref), custom_call_target="tpu_custom_call" | custom-call | tf_op jit(solution)/shard_map/damp/pallas_call | solution.py:712

commit v5 on v4

--- a/solution.py
+++ b/solution.py
@@ -100,6 +100,12 @@
     return result
 
 
+def tree_sum(terms):
+    while len(terms) > 1:
+        terms = [sum(terms[n + 1 : n + 2], terms[n]) for n in range(0, len(terms), 2)]
+    return terms[0]
+
+
 def from_above(cells, above=None):
     turned = pltpu.roll(cells, 1, 1)
     if above is None:
@@ -313,7 +319,7 @@
             return carry
 
         lax.fori_loop(0, 2 + (first == quad).astype(jnp.int32), body, 0)
-        if quad == 1:
+        if quad == 0:
             pl.semaphore_wait(relay.at[0], 2)
             tell(1, 2)
 
@@ -475,14 +481,11 @@
     for copy in rs:
         copy.wait_recv()
 
-    energy = rs_recv[0, 24:28, :]
-    for source in range(1, COMPS):
-        energy = energy + rs_recv[source, 24:28, :]
+    energy = tree_sum([rs_recv[source, 24:28, :] for source in range(COMPS)])
     energy = energy / K
     energy = jnp.concatenate([energy, energy], axis=0)
     square = energy * energy
-    plain = jnp.zeros((8, 128), jnp.float32)
-    shoaled = jnp.zeros((8, 128), jnp.float32)
+    parts = []
     for freq in range(NF):
         part = None
         for source in range(COMPS):
@@ -491,8 +494,9 @@
                 tile = rs_recv[source, 8 * slot : 8 * slot + 8, :]
                 part = tile if part is None else part + tile
         part = part / (1.0 + (2.0 * 1.1 ** (freq - (NF - 1))) * square)
-        plain = plain + part
-        shoaled = shoaled + (0.5 + 0.5 * freq / (NF - 1)) * part
+        parts.append(part)
+    plain = tree_sum(parts)
+    shoaled = tree_sum([(0.5 + 0.5 * freq / (NF - 1)) * part for freq, part in enumerate(parts)])
     turned = pltpu.roll(shoaled, 4, 0)
     final = plain / K
     stress_x = (turned + shoaled - 0.5 * plain) / K
@@ -608,7 +612,8 @@
         )
     surge = surge[8:72].reshape(8, 8, 128)
     reach = depth[...] + surge
-    damping = 1.0 / (1.0 + 4.0 * final / (reach * reach + 1.0))
+    depth_term = reach * reach + 1.0
+    damping = depth_term / (depth_term + 4.0 * final)
     for slot in range(3):
         factor_ref[slot] = rates[slot] * damping
     level_ref[...] = surge

time: 34.4 us -> 34.4 us (level)
  no operation moved by 1% of the time
where the time goes in v5:
time: 34.4 us; the launch traced here: 34.3 us
  Pallas kernels  33.7 us (98%)
  between operations  0.64 us (2%)
    pallas_call x1, Pallas kernels, local(): pl.pallas_call(step_kernel, out_shape=(pltpu.VMEM((LOCAL, *block), f32),...  32 us
    pallas_call x1, Pallas kernels, local(): pl.pallas_call(damp_kernel, out_shape=(jax.ShapeDtypeStruct((LOCAL, *bloc...  1.63 us

profile of v5, /device:TPU:1, one launch (start us, length us, event | category | flops | bytes accessed | tf_op | source)
XLA Modules:
  0.0 34.3 jit_solution(2397220048945231387)
XLA Ops:
  0.6 32.0 %wave_step.1 = (f32[81,8,8,128]{3,2,1,0:T(8,128)S(1)}, f32[3,8,8,128]{3,2,1,0:T(8,128)S(1)}, f32[8,8,128]{2,1,0:T(8,128)S(1)}) custom-call(f32[81,8,8,128]{3,2,1,0:T(8,128)} %bitcast.8, s32[8,8,128]{2,1,0:T(8,128)} %bitcast.9, s32[8,8,128]{2,1,0:T(8,128)} %bitcast.10, f32[8,8,128]{2,1,0:T(8,128)} %bitcast.11, f32[8,8,128]{2,1,0:T(8,128)} %bitcast.12, ...), custom_call_target="tpu_custom_call" | custom-call | tf_op jit(solution)/shard_map/wave_step/pallas_call | solution.py:650
  32.7 1.6 %damp.1 = (f32[81,8,8,128]{3,2,1,0:T(8,128)}, f32[8,8,128]{2,1,0:T(8,128)}) custom-call(f32[81,8,8,128]{3,2,1,0:T(8,128)S(1)} %get-tuple-element.7.grown_ref, f32[3,8,8,128]{3,2,1,0:T(8,128)S(1)} %get-tuple-element.8.factor_ref, f32[8,8,128]{2,1,0:T(8,128)S(1)} %get-tuple-element.9.level_ref), custom_call_target="tpu_custom_call" | custom-call | tf_op jit(solution)/shard_map/damp/pallas_call | solution.py:717

commit v6 on v5

--- a/solution.py
+++ b/solution.py
@@ -625,20 +625,22 @@
 def damp_kernel(grown_ref, factor_ref, level_ref, out_ref, level_out, x, out_sem, small_sem):
     first = lax.axis_index("comp") % 4
 
-    def store(group):
-        rows = pl.ds(9 * group, 9)
-        return pltpu.make_async_copy(x.at[rows], out_ref.at[rows], out_sem.at[group])
+    def store(part):
+        rows = pl.ds(27 * part, 27)
+        return pltpu.make_async_copy(x.at[rows], out_ref.at[rows], out_sem.at[part])
 
     surge = pltpu.make_async_copy(level_ref, level_out, small_sem.at[0])
-    surge.start()
     for group in range(GROUPS):
         factor = factor_ref[(first + group) // 4]
         for i in range(9):
             x[9 * group + i] = grown_ref[9 * group + i] * factor
-        store(group).start()
+        if group % 3 == 2:
+            store(group // 3).start()
+        if group == 2:
+            surge.start()
     surge.wait()
-    for group in range(GROUPS):
-        store(group).wait()
+    for part in range(3):
+        store(part).wait()
 
 
 def local(spectrum, land_mask, ice_mask, wind_u, wind_v, depth):
@@ -721,7 +723,7 @@
         out_specs=(anywhere, anywhere),
         scratch_shapes=[
             pltpu.VMEM((LOCAL, *block), f32),
-            dma((GROUPS,)),
+            dma((3,)),
             dma((1,)),
         ],
         compiler_params=pltpu.CompilerParams(vmem_limit_bytes=24 * 1024 * 1024),

time: 34.4 us -> 34.4 us (level)
  no operation moved by 1% of the time
where the time goes in v6:
time: 34.4 us; the launch traced here: 34.3 us
  Pallas kernels  33.7 us (98%)
  between operations  0.64 us (2%)
    pallas_call x1, Pallas kernels, local(): pl.pallas_call(step_kernel, out_shape=(pltpu.VMEM((LOCAL, *block), f32),...  32 us
    pallas_call x1, Pallas kernels, local(): pl.pallas_call(damp_kernel, out_shape=(jax.ShapeDtypeStruct((LOCAL, *bloc...  1.61 us

profile of v6, /device:TPU:1, one launch (start us, length us, event | category | flops | bytes accessed | tf_op | source)
XLA Modules:
  0.0 34.3 jit_solution(12009985078695870520)
XLA Ops:
  0.6 32.0 %wave_step.1 = (f32[81,8,8,128]{3,2,1,0:T(8,128)S(1)}, f32[3,8,8,128]{3,2,1,0:T(8,128)S(1)}, f32[8,8,128]{2,1,0:T(8,128)S(1)}) custom-call(f32[81,8,8,128]{3,2,1,0:T(8,128)} %bitcast.8, s32[8,8,128]{2,1,0:T(8,128)} %bitcast.9, s32[8,8,128]{2,1,0:T(8,128)} %bitcast.10, f32[8,8,128]{2,1,0:T(8,128)} %bitcast.11, f32[8,8,128]{2,1,0:T(8,128)} %bitcast.12, ...), custom_call_target="tpu_custom_call" | custom-call | tf_op jit(solution)/shard_map/wave_step/pallas_call | solution.py:652
  32.7 1.6 %damp.1 = (f32[81,8,8,128]{3,2,1,0:T(8,128)}, f32[8,8,128]{2,1,0:T(8,128)}) custom-call(f32[81,8,8,128]{3,2,1,0:T(8,128)S(1)} %get-tuple-element.7.grown_ref, f32[3,8,8,128]{3,2,1,0:T(8,128)S(1)} %get-tuple-element.8.factor_ref, f32[8,8,128]{2,1,0:T(8,128)S(1)} %get-tuple-element.9.level_ref), custom_call_target="tpu_custom_call" | custom-call | tf_op jit(solution)/shard_map/damp/pallas_call | solution.py:719
